TPU v7x, 32 devices: a whole 2x2x4 slice. The times are simulated.
32 devices in a mesh: section: 4 (over y, x), expert: 8 (over z, core).
Axes of the slice: x: 2, y: 2, z: 4, core: 2. Of those that a mesh axis runs over, the one named last changes fastest.
Arguments:
- fwd_arriving: bfloat16 [4, 256, 7168], P('section', 'expert'), may hold values from -6 to 6
- fwd_entering: bfloat16 [1, 256, 7168], P(None, 'expert'), may hold values from -6 to 6
- bwd_arriving: bfloat16 [4, 256, 7168], P('section', 'expert'), may hold values from -6 to 6
- bwd_entering: bfloat16 [1, 256, 7168], P(None, 'expert'), may hold values from -6 to 6
- saved_inputs: bfloat16 [4, 2, 256, 7168], P('section', None, 'expert'), may hold values from -6 to 6
- w_gate: bfloat16 [4, 8, 7168, 512], P('section', 'expert'), may hold values from -0.0625 to 0.0625
- w_up: bfloat16 [4, 8, 7168, 512], P('section', 'expert'), may hold values from -0.0625 to 0.0625
- w_down: bfloat16 [4, 8, 512, 7168], P('section', 'expert'), may hold values from -0.1875 to 0.1875
- route_ids: int32 [2, 4, 2, 256, 2], P(None, 'section', None, 'expert'), may hold values from 0 to 3, all different within a row; in each aligned block of 32 rows (0 to 31, 32 to 63, ..., all dimensions but the last counted through in order) at most 24 rows name the same one
- gate_levels: int32 [2, 4, 2, 256, 2], P(None, 'section', None, 'expert'), may hold values from 1 to 16
- token_counts: int32 [2, 5, 8], P(None, None, 'expert'), may hold values from 1 to 32, 224 in all within a row
Outputs:
- fwd_outputs: bfloat16 [4, 2, 256, 7168], P('section', None, 'expert')
- bwd_outputs: bfloat16 [4, 2, 256, 7168], P('section', None, 'expert')
Inputs may be any that keep to these rules, and one draw needn't show every extreme that they name: `route_ids`: each token names 2 different experts; among the 32 tokens of one device for one direction, section and step no expert is named by more than 24 tokens. `token_counts`: the first so many token slots of a device are live; for each direction and micro-batch the counts over the devices sum to 224 and the largest is 32.
All inputs are finite; a program needn't handle non-finite values.
Results may differ from a plain program's by a relative error of at most 0.009.
Values may be sent and summed in bfloat16 or wider, within the bound.
No kernel may reach another device: no remote copies, remote signals or barrier semaphores. Data moves between devices by JAX's collectives and lax.ppermute only.
A program may use at most 192 MiB of HBM per device.

v0:
```python
import jax
import jax.numpy as jnp
from jax import lax
from jax.sharding import PartitionSpec as P

SLICES = 2
TOPK = 2
TICKS = 2


def shifted(x, axis, by):
    devices = lax.axis_size(axis)
    pairs = [(i, i + by) for i in range(devices) if 0 <= i + by < devices]
    return lax.ppermute(x, axis, pairs)


def route_slots(route_row, level_row, live_count, experts_win, capacity):
    token_total = route_row.shape[0]
    topk_count = route_row.shape[1]
    live_mask = (jnp.arange(token_total, dtype=jnp.int32) < live_count).astype(jnp.int32)
    onehot = (
        route_row[:, :, None] == jnp.arange(experts_win, dtype=jnp.int32)[None, None, :]
    ).astype(jnp.int32)
    onehot = onehot * live_mask[:, None, None]
    onehot_flat = onehot.reshape(token_total * topk_count, experts_win)
    before = jnp.cumsum(onehot_flat, axis=0) - onehot_flat
    position = jnp.sum(before * onehot_flat, axis=1).reshape(token_total, topk_count)
    target = jnp.where(
        live_mask[:, None] > 0, route_row * capacity + position, experts_win * capacity
    )
    level_float = level_row.astype(jnp.float32)
    gate_weight = level_float / jnp.sum(level_float, axis=1, keepdims=True)
    return (target, gate_weight * live_mask[:, None].astype(jnp.float32))


def place_rows(row_block, target, experts_win, capacity):
    token_total, topk_count = target.shape
    features = row_block.shape[1]
    copies = jnp.broadcast_to(row_block[:, None, :], (token_total, topk_count, features)).reshape(
        token_total * topk_count, features
    )
    holder = jnp.zeros((experts_win * capacity + 1, features), row_block.dtype)
    placed = holder.at[target.reshape(-1)].set(copies)[: experts_win * capacity]
    return placed


def pack_rows(row_block, target, experts_win, capacity, piece_count):
    features = row_block.shape[1]
    placed = place_rows(row_block, target, experts_win, capacity)
    per_expert = placed.reshape(experts_win, 1, capacity, features)
    spread = jnp.broadcast_to(per_expert, (experts_win, piece_count, capacity, features))
    return spread.reshape(experts_win * piece_count, capacity, features)


def unpack_summed(summed, target, gate_weight):
    features = summed.shape[1]
    holder = jnp.concatenate([summed, jnp.zeros((1, features), jnp.float32)], axis=0)
    picked = holder[target]
    return jnp.sum(picked * gate_weight[:, :, None], axis=1)


def unpack_rows(returned, target, gate_weight, experts_win, capacity, piece_count):
    features = returned.shape[2]
    summed = (
        returned.reshape(experts_win, piece_count, capacity, features)
        .astype(jnp.float32)
        .sum(axis=1)
    )
    summed = summed.reshape(experts_win * capacity, features)
    return unpack_summed(summed, target, gate_weight)


def piece_forward(row_block, gate_piece, up_piece, down_piece):
    gate_pre = jnp.dot(row_block, gate_piece, preferred_element_type=jnp.float32)
    up_pre = jnp.dot(row_block, up_piece, preferred_element_type=jnp.float32)
    hidden = (jax.nn.silu(gate_pre) * up_pre).astype(jnp.bfloat16)
    return jnp.dot(hidden, down_piece, preferred_element_type=jnp.float32).astype(jnp.bfloat16)


def piece_backward(row_block, grad_block, gate_piece, up_piece, down_piece):
    gate_pre = jnp.dot(row_block, gate_piece, preferred_element_type=jnp.float32)
    up_pre = jnp.dot(row_block, up_piece, preferred_element_type=jnp.float32)
    d_hidden = jnp.einsum("rd,hd->rh", grad_block, down_piece, preferred_element_type=jnp.float32)
    sigmoid_gate = jax.nn.sigmoid(gate_pre)
    d_up = (d_hidden * gate_pre * sigmoid_gate).astype(jnp.bfloat16)
    d_gate = (d_hidden * up_pre * sigmoid_gate * (1.0 + gate_pre * (1.0 - sigmoid_gate))).astype(
        jnp.bfloat16
    )
    back_share = jnp.einsum("rh,dh->rd", d_gate, gate_piece, preferred_element_type=jnp.float32)
    back_share = back_share + jnp.einsum(
        "rh,dh->rd", d_up, up_piece, preferred_element_type=jnp.float32
    )
    return back_share.astype(jnp.bfloat16)


def local(
    fwd_arriving,
    fwd_entering,
    bwd_arriving,
    bwd_entering,
    saved_inputs,
    w_gate,
    w_up,
    w_down,
    route_ids,
    gate_levels,
    token_counts,
):
    section_index = lax.axis_index("section")
    section_total = lax.axis_size("section")
    piece_total = lax.axis_size("expert")
    experts_win = piece_total // SLICES
    tokens_dev = fwd_arriving.shape[1]
    capacity = min(tokens_dev, 3 * tokens_dev * TOPK // (2 * experts_win))
    gate_piece = w_gate[0, 0]
    up_piece = w_up[0, 0]
    down_piece = w_down[0, 0]
    fwd_state = fwd_arriving[0]
    bwd_state = bwd_arriving[0]
    fwd_list = []
    bwd_list = []
    for tick_index in range(TICKS):
        fwd_batch = tick_index - section_index + section_total - 1
        bwd_batch = tick_index + section_index
        fwd_live = lax.dynamic_index_in_dim(token_counts[0, :, 0], fwd_batch, 0, keepdims=False)
        bwd_live = lax.dynamic_index_in_dim(token_counts[1, :, 0], bwd_batch, 0, keepdims=False)
        fwd_target, fwd_gates = route_slots(
            route_ids[0, 0, tick_index],
            gate_levels[0, 0, tick_index],
            fwd_live,
            experts_win,
            capacity,
        )
        bwd_target, bwd_gates = route_slots(
            route_ids[1, 0, tick_index],
            gate_levels[1, 0, tick_index],
            bwd_live,
            experts_win,
            capacity,
        )
        fwd_send = pack_rows(fwd_state, fwd_target, experts_win, capacity, SLICES)
        saved_send = pack_rows(
            saved_inputs[0, tick_index], bwd_target, experts_win, capacity, SLICES
        )
        grad_send = pack_rows(bwd_state, bwd_target, experts_win, capacity, SLICES)
        forward_pieces = lax.all_to_all(fwd_send, "expert", split_axis=0, concat_axis=0, tiled=True)
        forward_sources, forward_slot_count, forward_features = forward_pieces.shape
        forward_piece_share = piece_forward(
            forward_pieces.reshape(forward_sources * forward_slot_count, forward_features),
            gate_piece,
            up_piece,
            down_piece,
        )
        fwd_returned = lax.all_to_all(
            forward_piece_share.reshape(forward_sources, forward_slot_count, forward_features),
            "expert",
            split_axis=0,
            concat_axis=0,
            tiled=True,
        )
        inputs_piece = lax.all_to_all(saved_send, "expert", split_axis=0, concat_axis=0, tiled=True)
        sources, slot_count, features = inputs_piece.shape
        piece_share = piece_backward(
            inputs_piece.reshape(sources * slot_count, features),
            lax.all_to_all(grad_send, "expert", split_axis=0, concat_axis=0, tiled=True).reshape(
                sources * slot_count, features
            ),
            gate_piece,
            up_piece,
            down_piece,
        )
        bwd_returned = lax.all_to_all(
            piece_share.reshape(sources, slot_count, features),
            "expert",
            split_axis=0,
            concat_axis=0,
            tiled=True,
        )
        fwd_added = unpack_rows(fwd_returned, fwd_target, fwd_gates, experts_win, capacity, SLICES)
        bwd_added = unpack_rows(bwd_returned, bwd_target, bwd_gates, experts_win, capacity, SLICES)
        fwd_result = (fwd_state.astype(jnp.float32) + fwd_added).astype(jnp.bfloat16)
        bwd_result = (bwd_state.astype(jnp.float32) + bwd_added).astype(jnp.bfloat16)
        fwd_list.append(fwd_result)
        bwd_list.append(bwd_result)
        if tick_index + 1 < TICKS:
            moved_forward = shifted(fwd_result, "section", 1)
            moved_backward = shifted(bwd_result, "section", -1)
            fwd_state = jnp.where(section_index == 0, fwd_entering[tick_index], moved_forward)
            bwd_state = jnp.where(
                section_index == section_total - 1, bwd_entering[tick_index], moved_backward
            )
    return (jnp.stack(fwd_list)[None], jnp.stack(bwd_list)[None])


def solution(mesh):
    return jax.shard_map(
        local,
        mesh=mesh,
        in_specs=(
            P("section", "expert", None),
            P(None, "expert", None),
            P("section", "expert", None),
            P(None, "expert", None),
            P("section", None, "expert", None),
            P("section", "expert", None, None),
            P("section", "expert", None, None),
            P("section", "expert", None, None),
            P(None, "section", None, "expert", None),
            P(None, "section", None, "expert", None),
            P(None, None, "expert"),
        ),
        out_specs=(P("section", None, "expert", None), P("section", None, "expert", None)),
        check_vma=False,
    )
```

profile of v0, /device:TPU:0, one launch (start us, length us, event | category | flops | bytes accessed | tf_op | source)
XLA Modules:
  0.0 717.4 jit_solution(11531843659929946978)
XLA Ops:
  14.4 6.5 all-to-all-start.5
  31.8 52.1 %all-to-all-done.5 = bf16[8,24,7168]{2,1,0:T(8,128)(2,1)S(1)} async-done(((bf16[8,24,7168]{2,1,0:T(8,128)(2,1)}), bf16[8,24,7168]{2,1,0:T(8,128)(2,1)S(1)}, u32[]{:S(2)}, u32[]{:S(2)}) %all-to-all-start.5) | async-done | bytes 2752544 | tf_op jit(solution)/shard_map/all_to_all | solution.py:161
  88.1 4.4 all-to-all-start.4
  97.0 58.7 %all-to-all-done.4 = bf16[8,24,7168]{2,1,0:T(8,128)(2,1)} async-done(((bf16[8,24,7168]{2,1,0:T(8,128)(2,1)}), bf16[8,24,7168]{2,1,0:T(8,128)(2,1)}, u32[]{:S(2)}, u32[]{:S(2)}) %all-to-all-start.4) | async-done | bytes 2752544 | tf_op jit(solution)/shard_map/all_to_all | solution.py:165
  178.7 45.4 %all-to-all-done.8 = bf16[8,24,7168]{2,1,0:T(8,128)(2,1)S(1)} async-done(((bf16[8,24,7168]{2,1,0:T(8,128)(2,1)}), bf16[8,24,7168]{2,1,0:T(8,128)(2,1)S(1)}, u32[]{:S(2)}, u32[]{:S(2)}) %all-to-all-start.8) | async-done | bytes 2752544 | tf_op jit(solution)/shard_map/all_to_all | solution.py:161
  224.2 4.3 broadcast_in_dim.176
  228.4 4.5 all-to-all-start
  232.9 6.3 fusion.24
  239.2 7.4 %fusion.4 = f32[192,512]{1,0:T(8,128)} fusion(bf16[192,7168]{1,0:T(8,128)(2,1)} %bitcast.36, bf16[1,1,512,7168]{3,2,1,0:T(8,128)(2,1)} %param.18), kind=kOutput, calls=%fused_computation.18 | convolution fusion | flops 1409286144 | bytes 10485760 | tf_op jit(solution)/shard_map/rd,hd->rh/dot_general | solution.py:83
  246.5 11.9 %fusion.22 = f32[192,7168]{1,0:T(8,128)} fusion(bf16[1,1,7168,512]{3,2,1,0:T(8,128)(2,1)} %param.16, f32[192,512]{1,0:T(8,128)} %fusion.4, bf16[192,7168]{1,0:T(8,128)(2,1)S(1)} %bitcast.246, bf16[1,1,7168,512]{3,2,1,0:T(8,128)(2,1)} %param.17, f32[192,512]{1,0:T(8,128)} %fusion.24), kind=kOutput, calls=%fused_computation.36 | convolution fusion | flops 2819555328 | bytes 23724032 | tf_op jit(solution)/shard_map/rh,dh->rd/dot_general | solution.py:89
  258.4 9.0 %fusion = bf16[192,7168]{1,0:T(8,128)(2,1)} fusion(f32[192,7168]{1,0:T(8,128)} %fusion.22, bf16[1,1,7168,512]{3,2,1,0:T(8,128)(2,1)} %param.17, f32[192,512]{1,0:T(8,128)} %fusion.4, f32[192,512]{1,0:T(8,128)} %fusion.24), kind=kOutput, calls=%fused_computation.12 | convolution fusion | flops 1412628480 | bytes 16384000 | tf_op jit(solution)/shard_map/rh,dh->rd/dot_general | solution.py:90
  267.4 28.6 %all-to-all-done = bf16[8,24,7168]{2,1,0:T(8,128)(2,1)} async-done(((bf16[8,24,7168]{2,1,0:T(8,128)(2,1)}), bf16[8,24,7168]{2,1,0:T(8,128)(2,1)}, u32[]{:S(2)}, u32[]{:S(2)}) %all-to-all-start) | async-done | bytes 2752544 | tf_op jit(solution)/shard_map/all_to_all | solution.py:146
  300.7 6.3 fusion.28
  307.0 10.8 %convolution_convert_fusion.1 = bf16[192,7168]{1,0:T(8,128)(2,1)} fusion(bf16[1,1,512,7168]{3,2,1,0:T(8,128)(2,1)} %param.18, bf16[192,7168]{1,0:T(8,128)(2,1)} %bitcast.6, bf16[1,1,7168,512]{3,2,1,0:T(8,128)(2,1)} %param.17, f32[192,512]{1,0:T(8,128)} %fusion.28), kind=kOutput, calls=%fused_computation.15 | convolution fusion | flops 2820538368 | bytes 20578304 | tf_op jit(solution)/shard_map/dot_general | solution.py:77
  317.8 45.0 %all-to-all-done.6 = bf16[8,24,7168]{2,1,0:T(8,128)(2,1)S(1)} async-done(((bf16[8,24,7168]{2,1,0:T(8,128)(2,1)}), bf16[8,24,7168]{2,1,0:T(8,128)(2,1)S(1)}, u32[]{:S(2)}, u32[]{:S(2)}) %all-to-all-start.6) | async-done | bytes 2752544 | tf_op jit(solution)/shard_map/all_to_all | solution.py:172
  362.8 4.7 all-to-all-start.1
  380.5 13.5 %collective-permute-done.1 = bf16[32,7168]{1,0:T(8,128)(2,1)S(1)} collective-permute-done((bf16[32,7168]{1,0:T(8,128)(2,1)S(1)}, bf16[32,7168]{1,0:T(8,128)(2,1)S(1)}, u32[]{:S(2)}, u32[]{:S(2)}) %collective-permute-start.1) | collective-permute-done | bytes 458784 | tf_op jit(solution)/shard_map/ppermute | solution.py:14
  398.0 32.6 %all-to-all-done.1 = bf16[8,24,7168]{2,1,0:T(8,128)(2,1)} async-done(((bf16[8,24,7168]{2,1,0:T(8,128)(2,1)}), bf16[8,24,7168]{2,1,0:T(8,128)(2,1)}, u32[]{:S(2)}, u32[]{:S(2)}) %all-to-all-start.1) | async-done | bytes 2752544 | tf_op jit(solution)/shard_map/all_to_all | solution.py:154
  432.6 4.8 all-to-all-start.7
  452.3 10.3 %collective-permute-done = bf16[32,7168]{1,0:T(8,128)(2,1)S(1)} collective-permute-done((bf16[32,7168]{1,0:T(8,128)(2,1)S(1)}, bf16[32,7168]{1,0:T(8,128)(2,1)S(1)}, u32[]{:S(2)}, u32[]{:S(2)}) %collective-permute-start) | collective-permute-done | bytes 458784 | tf_op jit(solution)/shard_map/ppermute | solution.py:14
  467.7 32.9 %all-to-all-done.7 = bf16[8,24,7168]{2,1,0:T(8,128)(2,1)} async-done(((bf16[8,24,7168]{2,1,0:T(8,128)(2,1)}), bf16[8,24,7168]{2,1,0:T(8,128)(2,1)}, u32[]{:S(2)}, u32[]{:S(2)}) %all-to-all-start.7) | async-done | bytes 2752544 | tf_op jit(solution)/shard_map/all_to_all | solution.py:165
  502.5 4.9 all-to-all-start.2
  507.4 5.4 fusion.20
  512.8 7.3 %fusion.2 = f32[192,512]{1,0:T(8,128)} fusion(bf16[192,7168]{1,0:T(8,128)(2,1)} %bitcast.53, bf16[1,1,512,7168]{3,2,1,0:T(8,128)(2,1)} %param.18), kind=kOutput, calls=%fused_computation.16 | convolution fusion | flops 1409286144 | bytes 10485760 | tf_op jit(solution)/shard_map/rd,hd->rh/dot_general | solution.py:83
  520.1 11.9 %fusion.18 = f32[192,7168]{1,0:T(8,128)} fusion(bf16[1,1,7168,512]{3,2,1,0:T(8,128)(2,1)} %param.16, f32[192,512]{1,0:T(8,128)} %fusion.2, bf16[192,7168]{1,0:T(8,128)(2,1)S(1)} %bitcast.244, bf16[1,1,7168,512]{3,2,1,0:T(8,128)(2,1)} %param.17, f32[192,512]{1,0:T(8,128)} %fusion.20), kind=kOutput, calls=%fused_computation.32 | convolution fusion | flops 2819555328 | bytes 23724032 | tf_op jit(solution)/shard_map/rh,dh->rd/dot_general | solution.py:89
  531.9 9.0 %fusion.1 = bf16[192,7168]{1,0:T(8,128)(2,1)} fusion(f32[192,7168]{1,0:T(8,128)} %fusion.18, bf16[1,1,7168,512]{3,2,1,0:T(8,128)(2,1)} %param.17, f32[192,512]{1,0:T(8,128)} %fusion.2, f32[192,512]{1,0:T(8,128)} %fusion.20), kind=kOutput, calls=%fused_computation.13 | convolution fusion | flops 1412628480 | bytes 16384000 | tf_op jit(solution)/shard_map/rh,dh->rd/dot_general | solution.py:90
  540.9 29.5 %all-to-all-done.2 = bf16[8,24,7168]{2,1,0:T(8,128)(2,1)} async-done(((bf16[8,24,7168]{2,1,0:T(8,128)(2,1)}), bf16[8,24,7168]{2,1,0:T(8,128)(2,1)}, u32[]{:S(2)}, u32[]{:S(2)}) %all-to-all-start.2) | async-done | bytes 2752544 | tf_op jit(solution)/shard_map/all_to_all | solution.py:146
  574.7 6.3 fusion.26
  581.0 10.8 %convolution_convert_fusion = bf16[192,7168]{1,0:T(8,128)(2,1)} fusion(bf16[1,1,512,7168]{3,2,1,0:T(8,128)(2,1)} %param.18, bf16[192,7168]{1,0:T(8,128)(2,1)} %bitcast.22, bf16[1,1,7168,512]{3,2,1,0:T(8,128)(2,1)} %param.17, f32[192,512]{1,0:T(8,128)} %fusion.26), kind=kOutput, calls=%fused_computation.14 | convolution fusion | flops 2820538368 | bytes 20578304 | tf_op jit(solution)/shard_map/dot_general | solution.py:77
  591.7 45.4 %all-to-all-done.9 = bf16[8,24,7168]{2,1,0:T(8,128)(2,1)S(1)} async-done(((bf16[8,24,7168]{2,1,0:T(8,128)(2,1)}), bf16[8,24,7168]{2,1,0:T(8,128)(2,1)S(1)}, u32[]{:S(2)}, u32[]{:S(2)}) %all-to-all-start.9) | async-done | bytes 2752544 | tf_op jit(solution)/shard_map/all_to_all | solution.py:172
  637.1 4.6 all-to-all-start.3
  654.1 50.8 %all-to-all-done.3 = bf16[8,24,7168]{2,1,0:T(8,128)(2,1)} async-done(((bf16[8,24,7168]{2,1,0:T(8,128)(2,1)}), bf16[8,24,7168]{2,1,0:T(8,128)(2,1)}, u32[]{:S(2)}, u32[]{:S(2)}) %all-to-all-start.3) | async-done | bytes 2752544 | tf_op jit(solution)/shard_map/all_to_all | solution.py:154
  (186 shorter events, 130.0 us)
Async XLA Ops:
  14.4 6.5 copy-start.6
  14.4 69.6 %all-to-all-start.5 = ((bf16[8,24,7168]{2,1,0:T(8,128)(2,1)}), bf16[8,24,7168]{2,1,0:T(8,128)(2,1)S(1)}, u32[]{:S(2)}, u32[]{:S(2)}) async-start(bf16[8,24,7168]{2,1,0:T(8,128)(2,1)} %bitcast.251), calls=%async_computation.5 | async-start | bytes 5505024 | tf_op jit(solution)/shard_map/all_to_all | solution.py:161
  84.0 4.2 copy-start.2
  88.1 67.5 %all-to-all-start.4 = ((bf16[8,24,7168]{2,1,0:T(8,128)(2,1)}), bf16[8,24,7168]{2,1,0:T(8,128)(2,1)}, u32[]{:S(2)}, u32[]{:S(2)}) async-start(bf16[8,24,7168]{2,1,0:T(8,128)(2,1)} %bitcast.248), calls=%async_computation.4 | async-start | bytes 5505024 | tf_op jit(solution)/shard_map/all_to_all | solution.py:165
  157.5 66.7 %all-to-all-start.8 = ((bf16[8,24,7168]{2,1,0:T(8,128)(2,1)}), bf16[8,24,7168]{2,1,0:T(8,128)(2,1)S(1)}, u32[]{:S(2)}, u32[]{:S(2)}) async-start(bf16[8,24,7168]{2,1,0:T(8,128)(2,1)} %bitcast.247), calls=%async_computation.8 | async-start | bytes 5505024 | tf_op jit(solution)/shard_map/all_to_all | solution.py:161
  224.2 4.3 copy-start
  228.4 67.6 %all-to-all-start = ((bf16[8,24,7168]{2,1,0:T(8,128)(2,1)}), bf16[8,24,7168]{2,1,0:T(8,128)(2,1)}, u32[]{:S(2)}, u32[]{:S(2)}) async-start(bf16[8,24,7168]{2,1,0:T(8,128)(2,1)} %bitcast.249), calls=%async_computation | async-start | bytes 5505024 | tf_op jit(solution)/shard_map/all_to_all | solution.py:146
  239.2 7.4 %copy-start.3 = (bf16[8,24,7168]{2,1,0:T(8,128)(2,1)S(1)}, bf16[8,24,7168]{2,1,0:T(8,128)(2,1)}, u32[]{:S(2)}) copy-start(bf16[8,24,7168]{2,1,0:T(8,128)(2,1)} %copy-done.2) | copy-start | bytes 8257540
  296.0 4.5 copy-start.15
  296.0 66.8 %all-to-all-start.6 = ((bf16[8,24,7168]{2,1,0:T(8,128)(2,1)}), bf16[8,24,7168]{2,1,0:T(8,128)(2,1)S(1)}, u32[]{:S(2)}, u32[]{:S(2)}) async-start(bf16[8,24,7168]{2,1,0:T(8,128)(2,1)} %bitcast.41), calls=%async_computation.6 | async-start | bytes 5505024 | tf_op jit(solution)/shard_map/all_to_all | solution.py:172
  362.8 7.3 %copy-start.16 = (s32[2,1,2,32,2]{3,4,2,1,0:T(2,128)S(1)}, s32[2,1,2,32,2]{3,4,2,1,0:T(2,128)}, u32[]{:S(2)}) copy-start(s32[2,1,2,32,2]{3,4,2,1,0:T(2,128)} %param.20) | copy-start | bytes 3076
  362.8 67.9 %all-to-all-start.1 = ((bf16[8,24,7168]{2,1,0:T(8,128)(2,1)}), bf16[8,24,7168]{2,1,0:T(8,128)(2,1)}, u32[]{:S(2)}, u32[]{:S(2)}) async-start(bf16[8,24,7168]{2,1,0:T(8,128)(2,1)} %bitcast.10), calls=%async_computation.1 | async-start | bytes 5505024 | tf_op jit(solution)/shard_map/all_to_all | solution.py:154
  375.8 18.2 %copy-start.14 = (bf16[1,32,7168]{2,1,0:T(8,128)(2,1)S(1)}, bf16[1,32,7168]{2,1,0:T(8,128)(2,1)}, u32[]{:S(2)}) copy-start(bf16[1,32,7168]{2,1,0:T(8,128)(2,1)} %param.14) | copy-start | bytes 1376260
  378.2 0.9 copy-start.4
  379.2 14.8 %collective-permute-start.1 = (bf16[32,7168]{1,0:T(8,128)(2,1)S(1)}, bf16[32,7168]{1,0:T(8,128)(2,1)S(1)}, u32[]{:S(2)}, u32[]{:S(2)}) collective-permute-start(bf16[32,7168]{1,0:T(8,128)(2,1)S(1)} %add_convert_fusion.1), channel_id=1, source_target_pairs={{8,0},{16,8},{24,16},{9,1},{17,9},{25,17},{10,2},{18,10},{26,18},{... | collective-permute-start | bytes 1376264 | tf_op jit(solution)/shard_map/ppermute | solution.py:14
  394.1 0.8 copy-start.8
  432.6 67.9 %all-to-all-start.7 = ((bf16[8,24,7168]{2,1,0:T(8,128)(2,1)}), bf16[8,24,7168]{2,1,0:T(8,128)(2,1)}, u32[]{:S(2)}, u32[]{:S(2)}) async-start(bf16[8,24,7168]{2,1,0:T(8,128)(2,1)} %bitcast.52), calls=%async_computation.7 | async-start | bytes 5505024 | tf_op jit(solution)/shard_map/all_to_all | solution.py:165
  442.9 5.9 copy-start.7
  447.8 0.9 copy-start.5
  448.8 13.8 %collective-permute-start = (bf16[32,7168]{1,0:T(8,128)(2,1)S(1)}, bf16[32,7168]{1,0:T(8,128)(2,1)S(1)}, u32[]{:S(2)}, u32[]{:S(2)}) collective-permute-start(bf16[32,7168]{1,0:T(8,128)(2,1)S(1)} %add_convert_fusion.3), channel_id=1, source_target_pairs={{0,8},{8,16},{16,24},{1,9},{9,17},{17,25},{2,10},{10,18},{18,26},{... | collective-permute-start | bytes 1376264 | tf_op jit(solution)/shard_map/ppermute | solution.py:14
  463.7 0.8 copy-start.10
  502.5 4.9 copy-start.1
  502.5 68.0 %all-to-all-start.2 = ((bf16[8,24,7168]{2,1,0:T(8,128)(2,1)}), bf16[8,24,7168]{2,1,0:T(8,128)(2,1)}, u32[]{:S(2)}, u32[]{:S(2)}) async-start(bf16[8,24,7168]{2,1,0:T(8,128)(2,1)} %bitcast.250), calls=%async_computation.2 | async-start | bytes 5505024 | tf_op jit(solution)/shard_map/all_to_all | solution.py:146
  570.5 66.7 %all-to-all-start.9 = ((bf16[8,24,7168]{2,1,0:T(8,128)(2,1)}), bf16[8,24,7168]{2,1,0:T(8,128)(2,1)S(1)}, u32[]{:S(2)}, u32[]{:S(2)}) async-start(bf16[8,24,7168]{2,1,0:T(8,128)(2,1)} %bitcast.58), calls=%async_computation.9 | async-start | bytes 5505024 | tf_op jit(solution)/shard_map/all_to_all | solution.py:172
  637.1 67.8 %all-to-all-start.3 = ((bf16[8,24,7168]{2,1,0:T(8,128)(2,1)}), bf16[8,24,7168]{2,1,0:T(8,128)(2,1)}, u32[]{:S(2)}, u32[]{:S(2)}) async-start(bf16[8,24,7168]{2,1,0:T(8,128)(2,1)} %bitcast.23), calls=%async_computation.3 | async-start | bytes 5505024 | tf_op jit(solution)/shard_map/all_to_all | solution.py:154
  648.3 4.9 copy-start.9
  710.0 5.0 copy-start.11
  712.5 2.6 copy-start.12
  712.5 2.6 copy-start.13
where the time goes:
time: 727 us; the launch traced here: 717 us
  waiting for transfers between devices  445 us (61%)
  matrix products  102 us (14%)
  local copies, waits for them, and re-layouts  85.3 us (12%)
  starting transfers between devices  50.2 us (7%)
  other arithmetic  33.2 us (5%)
    all_to_all x2, waiting for transfers between devices, local(): lax.all_to_all(saved_send, 'expert', split_axis=0, concat_axis=0, tiled=T...  97.6 us
    all_to_all x2, waiting for transfers between devices, local(): lax.all_to_all(grad_send, 'expert', split_axis=0, concat_axis=0, tiled=True)  91.6 us
    all_to_all x2, waiting for transfers between devices, local(): lax.all_to_all(piece_share.reshape(sources, slot_count, features), 'exper...  90.4 us
    all_to_all x2, waiting for transfers between devices, local(): lax.all_to_all(forward_piece_share.reshape(forward_sources, forward_slot_...  83.4 us
    all_to_all x2, waiting for transfers between devices, local(): lax.all_to_all(fwd_send, 'expert', split_axis=0, concat_axis=0, tiled=True)  58.2 us
    ppermute x2, waiting for transfers between devices, shifted(): return lax.ppermute(x, axis, pairs)  23.8 us
    dot_general x2, matrix products, piece_backward(): jnp.einsum('rh,dh->rd', d_gate, gate_piece, preferred_element_type=jnp.fl...  23.7 us
    dot_general x2, matrix products, piece_forward(): jnp.dot(hidden, down_piece, preferred_element_type=jnp.float32)  21.5 us
  transfers between devices with their start and end apart: 12, of which 12 were waited for; matrix products, arithmetic and copies ran while one was open for 25% of the time, Pallas kernels for 0%

commit v1 on v0

v1 whole, which is shorter than its diff:
```python
import jax
import jax.numpy as jnp
from jax import lax
from jax.experimental import pallas as pl
from jax.experimental.pallas import tpu as pltpu
from jax.sharding import PartitionSpec as P

SLICES = 2
TICKS = 2
LINE = 4
TILE = 1024
VMEM_LIMIT = 48 * 1024 * 1024
F32 = jnp.float32
BF16 = jnp.bfloat16
NT = (((1,), (1,)), ((), ()))
RIGHT = [(0, 1), (1, 2), (2, 3)]
LEFT = [(1, 0), (2, 1), (3, 2)]


def hop(x, chip_pairs):
    pairs = [(SLICES * a + c, SLICES * b + c) for a, b in chip_pairs for c in range(SLICES)]
    return lax.ppermute(x, "expert", pairs)


def swap(x):
    return lax.ppermute(x, "expert", [(i, i ^ 1) for i in range(lax.axis_size("expert"))])


def on_line():
    return lax.axis_size("expert") == LINE * SLICES


def slot_devices():
    devices = lax.axis_size("expert")
    if not on_line():
        return jnp.arange(devices)
    me = lax.axis_index("expert")
    chip, core = me // SLICES, me % SLICES
    chips = (chip - jnp.arange(LINE)) % LINE
    return jnp.concatenate([chips * SLICES + core, chips * SLICES + 1 - core])


def gather_rows(x):
    if not on_line():
        rows = lax.all_gather(x, "expert", axis=0, tiled=True)
        half = rows.shape[0] // 2
        return rows[:half], rows[half:]
    chip = lax.axis_index("expert") // SLICES
    right1 = hop(x, RIGHT)
    left1 = hop(x, LEFT)
    right2 = hop(right1, [(1, 2), (2, 3)])
    left2 = hop(left1, [(2, 1), (1, 0)])
    two = jnp.where(chip >= 2, right2, left2)
    far = hop(two, [(2, 3), (1, 0)])
    one = jnp.where(chip >= 1, right1, far)
    three = jnp.where(chip >= 3, far, left1)
    mine = jnp.concatenate([x, one, two, three], axis=0)
    return mine, swap(mine)


def scatter_sum(mine, other, residual):
    rows = residual.shape[0]
    if not on_line():
        total = lax.psum_scatter(
            jnp.concatenate([mine, other], axis=0), "expert", scatter_dimension=0, tiled=True
        )
        return (residual.astype(F32) + total.astype(F32)).astype(BF16)
    chip = lax.axis_index("expert") // SLICES
    part = (mine + swap(other)).reshape(LINE, rows, residual.shape[1])
    far = hop(jnp.where(chip < 2, part[1], part[3]), [(0, 1), (3, 2)])
    edge = hop(part[2], [(0, 1), (3, 2)])
    middle = hop(part[2] + far, [(1, 2), (2, 1)])
    right = hop(part[3] + jnp.where(chip == 1, edge, middle), RIGHT)
    left = hop(part[1] + jnp.where(chip == 2, edge, middle), LEFT)
    total = part[0].astype(F32) + right.astype(F32) + left.astype(F32)
    return (residual.astype(F32) + total).astype(BF16)


def stacked(a_ref, b_ref):
    return jnp.concatenate([a_ref[...], b_ref[...]], axis=0)


def split_store(value, a_ref, b_ref):
    half = a_ref.shape[0]
    a_ref[...] = value[:half].astype(a_ref.dtype)
    b_ref[...] = value[half:].astype(b_ref.dtype)


def forward_kernel(tiles, xm, xo, gate, wg, wu, wd, om, oo, acc_gate, acc_up, hidden):
    step = pl.program_id(0)

    @pl.when(step == 0)
    def _():
        acc_gate[...] = jnp.zeros_like(acc_gate)
        acc_up[...] = jnp.zeros_like(acc_up)

    @pl.when(step < tiles)
    def _():
        x = stacked(xm, xo)
        acc_gate[...] += jnp.dot(x, wg[...], preferred_element_type=F32)
        acc_up[...] += jnp.dot(x, wu[...], preferred_element_type=F32)

    @pl.when(step == tiles - 1)
    def _():
        pre = acc_gate[...]
        value = pre * jax.nn.sigmoid(pre) * acc_up[...] * gate[...]
        hidden[...] = value.astype(BF16)

    @pl.when(step >= tiles)
    def _():
        split_store(jnp.dot(hidden[...], wd[...], preferred_element_type=F32), om, oo)


def pre_kernel(tiles, xm, xo, wg, wu, pre_gate, pre_up):
    step = pl.program_id(0)
    x = stacked(xm, xo)

    @pl.when(step == 0)
    def _():
        pre_gate[...] = jnp.zeros_like(pre_gate)
        pre_up[...] = jnp.zeros_like(pre_up)

    pre_gate[...] += jnp.dot(x, wg[...], preferred_element_type=F32)
    pre_up[...] += jnp.dot(x, wu[...], preferred_element_type=F32)


def backward_kernel(
    tiles, gm, go, gate, pre_gate, pre_up, wd, wg, wu, om, oo, acc, d_gate, d_up
):
    step = pl.program_id(0)

    @pl.when(step == 0)
    def _():
        acc[...] = jnp.zeros_like(acc)

    @pl.when(step < tiles)
    def _():
        acc[...] += lax.dot_general(stacked(gm, go), wd[...], NT, preferred_element_type=F32)

    @pl.when(step == tiles - 1)
    def _():
        d_hidden = acc[...] * gate[...]
        pre = pre_gate[...]
        sig = jax.nn.sigmoid(pre)
        d_up[...] = (d_hidden * pre * sig).astype(BF16)
        d_gate[...] = (d_hidden * pre_up[...] * sig * (1.0 + pre * (1.0 - sig))).astype(BF16)

    @pl.when(step >= tiles)
    def _():
        value = lax.dot_general(d_gate[...], wg[...], NT, preferred_element_type=F32)
        value += lax.dot_general(d_up[...], wu[...], NT, preferred_element_type=F32)
        split_store(value, om, oo)


def specs(half, width, hid, tiles):
    first = lambda i: jnp.minimum(i, tiles - 1)
    second = lambda i: jnp.maximum(i - tiles, 0)
    return {
        "x": pl.BlockSpec((half, TILE), lambda i: (0, first(i))),
        "col1": pl.BlockSpec((TILE, hid), lambda i: (first(i), 0)),
        "col2": pl.BlockSpec((TILE, hid), lambda i: (second(i), 0)),
        "row1": pl.BlockSpec((hid, TILE), lambda i: (0, first(i))),
        "row2": pl.BlockSpec((hid, TILE), lambda i: (0, second(i))),
        "out": pl.BlockSpec((half, TILE), lambda i: (0, second(i))),
        "gate": pl.BlockSpec((2 * half, 1), lambda i: (0, 0)),
        "pre": pl.BlockSpec((2 * half, hid), lambda i: (0, 0)),
    }


def params():
    return pltpu.CompilerParams(vmem_limit_bytes=VMEM_LIMIT)


def cost(dots, half, width, hid, passes):
    return pl.CostEstimate(
        flops=2 * dots * 2 * half * width * hid,
        bytes_accessed=2 * width * (passes * hid + 4 * half),
        transcendentals=2 * half * hid,
    )


def forward_piece(xm, xo, gate, wg, wu, wd):
    half, width = xm.shape
    hid = wg.shape[1]
    tiles = width // TILE
    s = specs(half, width, hid, tiles)
    return pl.pallas_call(
        lambda *refs: forward_kernel(tiles, *refs),
        grid=(2 * tiles,),
        in_specs=[s["x"], s["x"], s["gate"], s["col1"], s["col1"], s["row2"]],
        out_specs=[s["out"], s["out"]],
        out_shape=[jax.ShapeDtypeStruct((half, width), BF16)] * 2,
        scratch_shapes=[
            pltpu.VMEM((2 * half, hid), F32),
            pltpu.VMEM((2 * half, hid), F32),
            pltpu.VMEM((2 * half, hid), BF16),
        ],
        compiler_params=params(),
        cost_estimate=cost(3, half, width, hid, 3),
        name="forward_piece",
    )(xm, xo, gate, wg, wu, wd)


def pre_piece(xm, xo, wg, wu):
    half, width = xm.shape
    hid = wg.shape[1]
    tiles = width // TILE
    s = specs(half, width, hid, tiles)
    return pl.pallas_call(
        lambda *refs: pre_kernel(tiles, *refs),
        grid=(tiles,),
        in_specs=[s["x"], s["x"], s["col1"], s["col1"]],
        out_specs=[s["pre"], s["pre"]],
        out_shape=[jax.ShapeDtypeStruct((2 * half, hid), F32)] * 2,
        compiler_params=params(),
        cost_estimate=cost(2, half, width, hid, 2),
        name="pre_piece",
    )(xm, xo, wg, wu)


def backward_piece(gm, go, gate, pre_gate, pre_up, wg, wu, wd):
    half, width = gm.shape
    hid = wg.shape[1]
    tiles = width // TILE
    s = specs(half, width, hid, tiles)
    return pl.pallas_call(
        lambda *refs: backward_kernel(tiles, *refs),
        grid=(2 * tiles,),
        in_specs=[s["x"], s["x"], s["gate"], s["pre"], s["pre"], s["row1"], s["col2"], s["col2"]],
        out_specs=[s["out"], s["out"]],
        out_shape=[jax.ShapeDtypeStruct((half, width), BF16)] * 2,
        scratch_shapes=[
            pltpu.VMEM((2 * half, hid), F32),
            pltpu.VMEM((2 * half, hid), BF16),
            pltpu.VMEM((2 * half, hid), BF16),
        ],
        compiler_params=params(),
        cost_estimate=cost(3, half, width, hid, 3),
        name="backward_piece",
    )(gm, go, gate, pre_gate, pre_up, wd, wg, wu)


def expert_gates(route_ids, gate_levels, token_counts):
    section = lax.axis_index("section")
    sections = lax.axis_size("section")
    devices = lax.axis_size("expert")
    experts = devices // SLICES
    routes, levels = route_ids[:, 0], gate_levels[:, 0].astype(F32)
    rows = routes.shape[2]
    ticks = jnp.arange(TICKS)
    batches = jnp.stack([ticks - section + sections - 1, ticks + section])
    counts = jnp.take_along_axis(token_counts[:, :, 0], batches, axis=1)
    live = jnp.arange(rows)[None, None, :] < counts[:, :, None]
    weights = levels / jnp.sum(levels, axis=-1, keepdims=True) * live[..., None].astype(F32)
    named = routes[..., None] == jnp.arange(experts)
    table = jnp.sum(jnp.where(named, weights[..., None], 0.0), axis=3)
    everyone = lax.all_gather(table, "expert", axis=0, tiled=False)
    expert = lax.axis_index("expert") // SLICES
    column = lax.dynamic_index_in_dim(everyone, expert, 4, keepdims=False)
    column = column[slot_devices()]
    return jnp.moveaxis(column, 0, 2).reshape(2, TICKS, devices * rows, 1)


def local(
    fwd_arriving,
    fwd_entering,
    bwd_arriving,
    bwd_entering,
    saved_inputs,
    w_gate,
    w_up,
    w_down,
    route_ids,
    gate_levels,
    token_counts,
):
    section = lax.axis_index("section")
    sections = lax.axis_size("section")
    wg, wu, wd = w_gate[0, 0], w_up[0, 0], w_down[0, 0]
    gates = expert_gates(route_ids, gate_levels, token_counts)
    ahead = [(i, (i + 1) % sections) for i in range(sections)]
    back = [(i, (i - 1) % sections) for i in range(sections)]
    fwd_state, bwd_state = fwd_arriving[0], bwd_arriving[0]
    fwd_list, bwd_list = [], []
    for tick in range(TICKS):
        fm, fo = gather_rows(fwd_state)
        sm, so = gather_rows(saved_inputs[0, tick])
        gm, go = gather_rows(bwd_state)
        fwd_out = forward_piece(fm, fo, gates[0, tick], wg, wu, wd)
        pre_gate, pre_up = pre_piece(sm, so, wg, wu)
        bwd_out = backward_piece(gm, go, gates[1, tick], pre_gate, pre_up, wg, wu, wd)
        fwd_state = scatter_sum(*fwd_out, fwd_state)
        bwd_state = scatter_sum(*bwd_out, bwd_state)
        fwd_list.append(fwd_state)
        bwd_list.append(bwd_state)
        if tick + 1 < TICKS:
            fwd_state = lax.ppermute(
                jnp.where(section == sections - 1, fwd_entering[tick], fwd_state), "section", ahead
            )
            bwd_state = lax.ppermute(
                jnp.where(section == 0, bwd_entering[tick], bwd_state), "section", back
            )
    return jnp.stack(fwd_list)[None], jnp.stack(bwd_list)[None]


def solution(mesh):
    return jax.shard_map(
        local,
        mesh=mesh,
        in_specs=(
            P("section", "expert", None),
            P(None, "expert", None),
            P("section", "expert", None),
            P(None, "expert", None),
            P("section", None, "expert", None),
            P("section", "expert", None, None),
            P("section", "expert", None, None),
            P("section", "expert", None, None),
            P(None, "section", None, "expert", None),
            P(None, "section", None, "expert", None),
            P(None, None, "expert"),
        ),
        out_specs=(P("section", None, "expert", None), P("section", None, "expert", None)),
        check_vma=False,
    )
```

time: 727 us -> 427 us (0.59)
  waiting for transfers between devices: 445 us -> 185 us
  matrix products: 102 us -> 0 us
  Pallas kernels: 0 us -> 87.1 us
  local copies, waits for them, and re-layouts: 85.3 us -> 6.04 us
  starting transfers between devices: 50.2 us -> 114 us
  other arithmetic: 33.2 us -> 15.8 us
  blocking collectives: 0 us -> 14 us
    all_to_all x10 -> x0, waiting for transfers between devices: 421 us -> none  [the longest x2 97.6 us: local(): lax.all_to_all(saved_send, 'expert', split_axis=0, concat_axis=0, tiled=T...]
    ppermute x2 -> x62, waiting for transfers between devices: 23.8 us -> 185 us  [the longest x50 180 us: hop(): return lax.ppermute(x, 'expert', pairs)]
    ppermute x2 -> x62, starting transfers between devices: 4.72 us -> 114 us  [the longest x50 109 us: hop(): return lax.ppermute(x, 'expert', pairs)]
    dot_general x12 -> x0, matrix products: 102 us -> none  [the longest x2 23.7 us: piece_backward(): jnp.einsum('rh,dh->rd', d_gate, gate_piece, preferred_element_type=jnp.fl...]
    pallas_call x0 -> x6, Pallas kernels: none -> 87.1 us  [the longest x2 34.9 us: backward_piece(): pl.pallas_call(lambda *refs: backward_kernel(tiles, *refs), grid=(2 * til...]
    all_to_all x10 -> x0, starting transfers between devices: 45.5 us -> none  [the longest x2 10.1 us: local(): lax.all_to_all(saved_send, 'expert', split_axis=0, concat_axis=0, tiled=T...]
    broadcast_in_dim x21 -> x0, local copies, waits for them, and re-layouts: 25.4 us -> none  [the longest x6 16 us: pack_rows(): jnp.broadcast_to(per_expert, (experts_win, piece_count, capacity, features))]
    gather x8 -> x4, local copies, waits for them, and re-layouts: 19.3 us -> 1.39 us  [the longest x3 0.81 us: expert_gates(): counts = jnp.take_along_axis(token_counts[:, :, 0], batches, axis=1)]
  transfers between devices with their start and end apart: 12 -> 62, of which waited for: 12 -> 31; matrix products, arithmetic and copies ran while one was open for 25% -> 4% of each run, Pallas kernels for 0% -> 21%
where the time goes in v1:
time: 427 us; the launch traced here: 424 us
  waiting for transfers between devices  185 us (43%)
  starting transfers between devices  114 us (27%)
  Pallas kernels  87.1 us (20%)
  other arithmetic  15.8 us (4%)
  blocking collectives  14 us (3%)
  local copies, waits for them, and re-layouts  6.04 us (1%)
    ppermute x50, waiting for transfers between devices, hop(): return lax.ppermute(x, 'expert', pairs)  180 us
    ppermute x50, starting transfers between devices, hop(): return lax.ppermute(x, 'expert', pairs)  109 us
    pallas_call x2, Pallas kernels, backward_piece(): pl.pallas_call(lambda *refs: backward_kernel(tiles, *refs), grid=(2 * til...  34.9 us
    pallas_call x2, Pallas kernels, forward_piece(): pl.pallas_call(lambda *refs: forward_kernel(tiles, *refs), grid=(2 * tile...  32.8 us
    pallas_call x2, Pallas kernels, pre_piece(): pl.pallas_call(lambda *refs: pre_kernel(tiles, *refs), grid=(tiles,), in_...  19.4 us
    all_gather x1, blocking collectives, expert_gates(): everyone = lax.all_gather(table, 'expert', axis=0, tiled=False)  14 us
  transfers between devices with their start and end apart: 62, of which 31 were waited for; matrix products, arithmetic and copies ran while one was open for 4% of the time, Pallas kernels for 21%

profile of v1, /device:TPU:0, one launch (start us, length us, event | category | flops | bytes accessed | tf_op | source)
XLA Modules:
  0.0 424.3 jit_solution(14621004548586515977)
XLA Ops:
  2.0 5.7 %collective-permute-start.31 = (bf16[32,7168]{1,0:T(8,128)(2,1)S(1)}, bf16[32,7168]{1,0:T(8,128)(2,1)}, u32[]{:S(2)}, u32[]{:S(2)}) collective-permute-start(bf16[32,7168]{1,0:T(8,128)(2,1)S(1)} %get-tuple-element.47), channel_id=1, source_target_pairs={{0,2},{1,3},{2,4},{3,5},{4,6},{5,7},{8,10},{9,11},{10,12},{11,13},... | collective-permute-start | bytes 1376264 | tf_op jit(solution)/shard_map/ppermute | solution.py:22
  9.0 5.3 %collective-permute-start.25 = (bf16[32,7168]{1,0:T(8,128)(2,1)S(1)}, bf16[32,7168]{1,0:T(8,128)(2,1)}, u32[]{:S(2)}, u32[]{:S(2)}) collective-permute-start(bf16[32,7168]{1,0:T(8,128)(2,1)S(1)} %bitcast.74), channel_id=1, source_target_pairs={{0,2},{1,3},{2,4},{3,5},{4,6},{5,7},{8,10},{9,11},{10,12},{11,13},... | collective-permute-start | bytes 1376264 | tf_op jit(solution)/shard_map/ppermute | solution.py:22
  15.6 4.6 %collective-permute-start = (bf16[32,7168]{1,0:T(8,128)(2,1)S(1)}, bf16[32,7168]{1,0:T(8,128)(2,1)S(1)}, u32[]{:S(2)}, u32[]{:S(2)}) collective-permute-start(bf16[32,7168]{1,0:T(8,128)(2,1)S(1)} %bitcast.77), channel_id=1, source_target_pairs={{0,2},{1,3},{2,4},{3,5},{4,6},{5,7},{8,10},{9,11},{10,12},{11,13},... | collective-permute-start | bytes 1376264 | tf_op jit(solution)/shard_map/ppermute | solution.py:22
  37.1 5.5 %collective-permute-done.34 = bf16[32,7168]{1,0:T(8,128)(2,1)S(1)} collective-permute-done((bf16[32,7168]{1,0:T(8,128)(2,1)}, bf16[32,7168]{1,0:T(8,128)(2,1)S(1)}, u32[]{:S(2)}, u32[]{:S(2)}) %collective-permute-start.34) | collective-permute-done | bytes 458784 | tf_op jit(solution)/shard_map/ppermute | solution.py:22
  45.3 5.7 %collective-permute-done.2 = bf16[32,7168]{1,0:T(8,128)(2,1)S(1)} collective-permute-done((bf16[32,7168]{1,0:T(8,128)(2,1)S(1)}, bf16[32,7168]{1,0:T(8,128)(2,1)S(1)}, u32[]{:S(2)}, u32[]{:S(2)}) %collective-permute-start.2) | collective-permute-done | bytes 458784 | tf_op jit(solution)/shard_map/ppermute | solution.py:22
  53.0 13.8 %collective-permute-done.28 = bf16[32,7168]{1,0:T(8,128)(2,1)S(1)} collective-permute-done((bf16[32,7168]{1,0:T(8,128)(2,1)}, bf16[32,7168]{1,0:T(8,128)(2,1)S(1)}, u32[]{:S(2)}, u32[]{:S(2)}) %collective-permute-start.28) | collective-permute-done | bytes 458784 | tf_op jit(solution)/shard_map/ppermute | solution.py:22
  69.5 17.0 %collective-permute-done.3 = bf16[32,7168]{1,0:T(8,128)(2,1)S(1)} collective-permute-done((bf16[32,7168]{1,0:T(8,128)(2,1)S(1)}, bf16[32,7168]{1,0:T(8,128)(2,1)S(1)}, u32[]{:S(2)}, u32[]{:S(2)}) %collective-permute-start.3) | collective-permute-done | bytes 458784 | tf_op jit(solution)/shard_map/ppermute | solution.py:22
  87.9 8.5 %collective-permute-done.35 = bf16[32,7168]{1,0:T(8,128)(2,1)S(1)} collective-permute-done((bf16[32,7168]{1,0:T(8,128)(2,1)S(1)}, bf16[32,7168]{1,0:T(8,128)(2,1)S(1)}, u32[]{:S(2)}, u32[]{:S(2)}) %collective-permute-start.35) | collective-permute-done | bytes 458784 | tf_op jit(solution)/shard_map/ppermute | solution.py:22
  97.7 8.5 %collective-permute-done.29 = bf16[32,7168]{1,0:T(8,128)(2,1)S(1)} collective-permute-done((bf16[32,7168]{1,0:T(8,128)(2,1)S(1)}, bf16[32,7168]{1,0:T(8,128)(2,1)S(1)}, u32[]{:S(2)}, u32[]{:S(2)}) %collective-permute-start.29) | collective-permute-done | bytes 458784 | tf_op jit(solution)/shard_map/ppermute | solution.py:22
  114.3 14.0 %all-gather = f32[16,2,32,4]{2,3,1,0:T(4,128)S(1)} all-gather(f32[2,2,32,4]{2,3,1,0:T(4,128)S(1)} %select_reduce_fusion), channel_id=2, replica_groups=mesh['section'=4,'expert'=8] {'expert'}, dimensions={0}, use_global_device_ids=true | all-gather | bytes 18432 | tf_op jit(solution)/shard_map/all_gather | solution.py:257
  131.6 9.9 %pre_piece.2 = (f32[256,512]{1,0:T(8,128)S(1)}, f32[256,512]{1,0:T(8,128)S(1)}) custom-call(bf16[128,7168]{1,0:T(8,128)(2,1)S(1)} %pad_maximum_fusion.3.refs_0_, bf16[128,7168]{1,0:T(8,128)(2,1)} %collective-permute-done.36.refs_1_, bf16[7168,512]{1,0:T(8,128)(2,1)} %bitcast.58, bf16[7168,512]{1,0:T(8,128)(2,1)} %bitcast.64), custom_call_target="tpu_custom_call" | custom-call | flops 3758096384 | bytes 22020096 | tf_op jit(solution)/shard_map/pre_piece/pallas_call | solution.py:209
  141.5 17.0 %backward_piece.2 = (bf16[128,7168]{1,0:T(8,128)(2,1)S(1)}, bf16[128,7168]{1,0:T(8,128)(2,1)S(1)}) custom-call(bf16[128,7168]{1,0:T(8,128)(2,1)} %pad_maximum_fusion.2.refs_0_, bf16[128,7168]{1,0:T(8,128)(2,1)} %collective-permute-done.30.refs_1_, f32[256,1]{1,0:T(8,128)S(1)} %copy.42.refs_2_, f32[256,512]{1,0:T(8,128)S(1)} %get-tuple-element.18.refs_3_, ...), custom_call_target="tpu_custom_call" | custom-call | flops 5637144576 | bytes 29360128 | tf_op jit(solution)/shard_map/backward_piece/pallas_call | solution.py:226
  158.9 16.4 %forward_piece.2 = (bf16[128,7168]{1,0:T(8,128)(2,1)S(1)}, bf16[128,7168]{1,0:T(8,128)(2,1)S(1)}) custom-call(bf16[128,7168]{1,0:T(8,128)(2,1)} %pad_maximum_fusion.refs_0_, bf16[128,7168]{1,0:T(8,128)(2,1)} %collective-permute-done.5.refs_1_, f32[256,1]{1,0:T(8,128)S(1)} %copy.40.refs_2_, bf16[7168,512]{1,0:T(8,128)(2,1)} %bitcast.60, ...), custom_call_target="tpu_custom_call" | custom-call | flops 5637144576 | bytes 29360128 | tf_op jit(solution)/shard_map/forward_piece/pallas_call | solution.py:187
  177.4 5.0 %collective-permute-start.39 = (bf16[32,7168]{1,0:T(8,128)(2,1)S(1)}, bf16[32,7168]{1,0:T(8,128)(2,1)S(1)}, u32[]{:S(2)}, u32[]{:S(2)}) collective-permute-start(bf16[32,7168]{1,0:T(8,128)(2,1)S(1)} %broadcast_select_fusion.1), channel_id=1, source_target_pairs={{0,2},{1,3},{6,4},{7,5},{8,10},{9,11},{14,12},{15,13},{16,18},{17,... | collective-permute-start | bytes 1376264 | tf_op jit(solution)/shard_map/ppermute | solution.py:22
  184.4 8.8 %collective-permute-done.39 = bf16[32,7168]{1,0:T(8,128)(2,1)S(1)} collective-permute-done((bf16[32,7168]{1,0:T(8,128)(2,1)S(1)}, bf16[32,7168]{1,0:T(8,128)(2,1)S(1)}, u32[]{:S(2)}, u32[]{:S(2)}) %collective-permute-start.39) | collective-permute-done | bytes 458784 | tf_op jit(solution)/shard_map/ppermute | solution.py:22
  198.5 4.6 %collective-permute-done.8 = bf16[32,7168]{1,0:T(8,128)(2,1)S(1)} collective-permute-done((bf16[32,7168]{1,0:T(8,128)(2,1)S(1)}, bf16[32,7168]{1,0:T(8,128)(2,1)S(1)}, u32[]{:S(2)}, u32[]{:S(2)}) %collective-permute-start.8) | collective-permute-done | bytes 458784 | tf_op jit(solution)/shard_map/ppermute | solution.py:22
  208.3 4.6 %collective-permute-done.38 = bf16[32,7168]{1,0:T(8,128)(2,1)S(1)} collective-permute-done((bf16[32,7168]{1,0:T(8,128)(2,1)S(1)}, bf16[32,7168]{1,0:T(8,128)(2,1)S(1)}, u32[]{:S(2)}, u32[]{:S(2)}) %collective-permute-start.38) | collective-permute-done | bytes 458784 | tf_op jit(solution)/shard_map/ppermute | solution.py:22
  236.1 5.4 %collective-permute-done.10 = bf16[32,7168]{1,0:T(8,128)(2,1)S(1)} collective-permute-done((bf16[32,7168]{1,0:T(8,128)(2,1)S(1)}, bf16[32,7168]{1,0:T(8,128)(2,1)S(1)}, u32[]{:S(2)}, u32[]{:S(2)}) %collective-permute-start.10) | collective-permute-done | bytes 458784 | tf_op jit(solution)/shard_map/ppermute | solution.py:22
  263.1 5.4 %collective-permute-done.13 = bf16[32,7168]{1,0:T(8,128)(2,1)S(1)} collective-permute-done((bf16[32,7168]{1,0:T(8,128)(2,1)S(1)}, bf16[32,7168]{1,0:T(8,128)(2,1)S(1)}, u32[]{:S(2)}, u32[]{:S(2)}) %collective-permute-start.13) | collective-permute-done | bytes 458784 | tf_op jit(solution)/shard_map/ppermute | solution.py:22
  269.4 5.5 %collective-permute-done.15 = bf16[32,7168]{1,0:T(8,128)(2,1)S(1)} collective-permute-done((bf16[32,7168]{1,0:T(8,128)(2,1)S(1)}, bf16[32,7168]{1,0:T(8,128)(2,1)S(1)}, u32[]{:S(2)}, u32[]{:S(2)}) %collective-permute-start.15) | collective-permute-done | bytes 458784 | tf_op jit(solution)/shard_map/ppermute | solution.py:22
  276.2 8.5 %collective-permute-done.47 = bf16[32,7168]{1,0:T(8,128)(2,1)S(1)} collective-permute-done((bf16[32,7168]{1,0:T(8,128)(2,1)S(1)}, bf16[32,7168]{1,0:T(8,128)(2,1)S(1)}, u32[]{:S(2)}, u32[]{:S(2)}) %collective-permute-start.47) | collective-permute-done | bytes 458784 | tf_op jit(solution)/shard_map/ppermute | solution.py:22
  286.1 8.5 %collective-permute-done.16 = bf16[32,7168]{1,0:T(8,128)(2,1)S(1)} collective-permute-done((bf16[32,7168]{1,0:T(8,128)(2,1)S(1)}, bf16[32,7168]{1,0:T(8,128)(2,1)S(1)}, u32[]{:S(2)}, u32[]{:S(2)}) %collective-permute-start.16) | collective-permute-done | bytes 458784 | tf_op jit(solution)/shard_map/ppermute | solution.py:22
  296.0 8.5 %collective-permute-done.48 = bf16[32,7168]{1,0:T(8,128)(2,1)S(1)} collective-permute-done((bf16[32,7168]{1,0:T(8,128)(2,1)S(1)}, bf16[32,7168]{1,0:T(8,128)(2,1)S(1)}, u32[]{:S(2)}, u32[]{:S(2)}) %collective-permute-start.48) | collective-permute-done | bytes 458784 | tf_op jit(solution)/shard_map/ppermute | solution.py:22
  304.8 7.5 %collective-permute-done.17 = bf16[32,7168]{1,0:T(8,128)(2,1)S(1)} collective-permute-done((bf16[32,7168]{1,0:T(8,128)(2,1)S(1)}, bf16[32,7168]{1,0:T(8,128)(2,1)S(1)}, u32[]{:S(2)}, u32[]{:S(2)}) %collective-permute-start.17) | collective-permute-done | bytes 458784 | tf_op jit(solution)/shard_map/ppermute | solution.py:22
  312.6 9.6 %pre_piece.3 = (f32[256,512]{1,0:T(8,128)S(1)}, f32[256,512]{1,0:T(8,128)S(1)}) custom-call(bf16[128,7168]{1,0:T(8,128)(2,1)S(1)} %pad_maximum_fusion.5.refs_0_, bf16[128,7168]{1,0:T(8,128)(2,1)S(1)} %collective-permute-done.55.refs_1_, bf16[7168,512]{1,0:T(8,128)(2,1)} %bitcast.61, bf16[7168,512]{1,0:T(8,128)(2,1)} %bitcast.67), custom_call_target="tpu_custom_call" | custom-call | flops 3758096384 | bytes 22020096 | tf_op jit(solution)/shard_map/pre_piece/pallas_call | solution.py:209
  323.5 17.9 %backward_piece.3 = (bf16[128,7168]{1,0:T(8,128)(2,1)S(1)}, bf16[128,7168]{1,0:T(8,128)(2,1)}) custom-call(bf16[128,7168]{1,0:T(8,128)(2,1)} %copy-done.4, bf16[128,7168]{1,0:T(8,128)(2,1)} %copy-done.5, f32[256,1]{1,0:T(8,128)S(1)} %copy.43.refs_2_, f32[256,512]{1,0:T(8,128)S(1)} %get-tuple-element.22.refs_3_, f32[256,512]{1,0:T(8,128)S(1)} %get-tuple-element.23.refs_4_, ...), custom_call_target="tpu_custom_call" | custom-call | flops 5637144576 | bytes 29360128 | tf_op jit(solution)/shard_map/backward_piece/pallas_call | solution.py:226
  343.3 16.4 %forward_piece.3 = (bf16[128,7168]{1,0:T(8,128)(2,1)S(1)}, bf16[128,7168]{1,0:T(8,128)(2,1)S(1)}) custom-call(bf16[128,7168]{1,0:T(8,128)(2,1)S(1)} %pad_maximum_fusion.1.refs_0_, bf16[128,7168]{1,0:T(8,128)(2,1)} %collective-permute-done.18.refs_1_, f32[256,1]{1,0:T(8,128)S(1)} %copy.41.refs_2_, bf16[7168,512]{1,0:T(8,128)(2,1)} %bitcast.63, ...), custom_call_target="tpu_custom_call" | custom-call | flops 5637144576 | bytes 29360128 | tf_op jit(solution)/shard_map/forward_piece/pallas_call | solution.py:187
  365.5 8.7 %collective-permute-done.58 = bf16[32,7168]{1,0:T(8,128)(2,1)S(1)} collective-permute-done((bf16[32,7168]{1,0:T(8,128)(2,1)S(1)}, bf16[32,7168]{1,0:T(8,128)(2,1)S(1)}, u32[]{:S(2)}, u32[]{:S(2)}) %collective-permute-start.58) | collective-permute-done | bytes 458784 | tf_op jit(solution)/shard_map/ppermute | solution.py:22
  379.4 4.6 %collective-permute-done.21 = bf16[32,7168]{1,0:T(8,128)(2,1)S(1)} collective-permute-done((bf16[32,7168]{1,0:T(8,128)(2,1)S(1)}, bf16[32,7168]{1,0:T(8,128)(2,1)S(1)}, u32[]{:S(2)}, u32[]{:S(2)}) %collective-permute-start.21) | collective-permute-done | bytes 458784 | tf_op jit(solution)/shard_map/ppermute | solution.py:22
  389.2 4.6 %collective-permute-done.57 = bf16[32,7168]{1,0:T(8,128)(2,1)S(1)} collective-permute-done((bf16[32,7168]{1,0:T(8,128)(2,1)S(1)}, bf16[32,7168]{1,0:T(8,128)(2,1)S(1)}, u32[]{:S(2)}, u32[]{:S(2)}) %collective-permute-start.57) | collective-permute-done | bytes 458784 | tf_op jit(solution)/shard_map/ppermute | solution.py:22
  394.0 4.5 %collective-permute-start.60 = (bf16[32,7168]{1,0:T(8,128)(2,1)S(1)}, bf16[32,7168]{1,0:T(8,128)(2,1)S(1)}, u32[]{:S(2)}, u32[]{:S(2)}) collective-permute-start(bf16[32,7168]{1,0:T(8,128)(2,1)S(1)} %get-tuple-element.30), channel_id=1, source_target_pairs={{0,2},{1,3},{2,4},{3,5},{4,6},{5,7},{8,10},{9,11},{10,12},{11,13},... | collective-permute-start | bytes 1376264 | tf_op jit(solution)/shard_map/ppermute | solution.py:22
  414.8 8.3 %collective-permute-done.23 = bf16[32,7168]{1,0:T(8,128)(2,1)S(1)} collective-permute-done((bf16[32,7168]{1,0:T(8,128)(2,1)S(1)}, bf16[32,7168]{1,0:T(8,128)(2,1)S(1)}, u32[]{:S(2)}, u32[]{:S(2)}) %collective-permute-start.23) | collective-permute-done | bytes 458784 | tf_op jit(solution)/shard_map/ppermute | solution.py:22
  (205 shorter events, 143.7 us)
Async XLA Ops:
  9.0 18.7 %collective-permute-start.25 = (bf16[32,7168]{1,0:T(8,128)(2,1)S(1)}, bf16[32,7168]{1,0:T(8,128)(2,1)}, u32[]{:S(2)}, u32[]{:S(2)}) collective-permute-start(bf16[32,7168]{1,0:T(8,128)(2,1)S(1)} %bitcast.74), channel_id=1, source_target_pairs={{0,2},{1,3},{2,4},{3,5},{4,6},{5,7},{8,10},{9,11},{10,12},{11,13},... | collective-permute-start | bytes 1376264 | tf_op jit(solution)/shard_map/ppermute | solution.py:22
  14.3 18.6 %collective-permute-start.27 = (bf16[32,7168]{1,0:T(8,128)(2,1)S(1)}, bf16[32,7168]{1,0:T(8,128)(2,1)}, u32[]{:S(2)}, u32[]{:S(2)}) collective-permute-start(bf16[32,7168]{1,0:T(8,128)(2,1)S(1)} %bitcast.75), channel_id=1, source_target_pairs={{2,0},{3,1},{4,2},{5,3},{6,4},{7,5},{10,8},{11,9},{12,10},{13,11},... | collective-permute-start | bytes 1376264 | tf_op jit(solution)/shard_map/ppermute | solution.py:22
  15.6 28.4 %collective-permute-start = (bf16[32,7168]{1,0:T(8,128)(2,1)S(1)}, bf16[32,7168]{1,0:T(8,128)(2,1)S(1)}, u32[]{:S(2)}, u32[]{:S(2)}) collective-permute-start(bf16[32,7168]{1,0:T(8,128)(2,1)S(1)} %bitcast.77), channel_id=1, source_target_pairs={{0,2},{1,3},{2,4},{3,5},{4,6},{5,7},{8,10},{9,11},{10,12},{11,13},... | collective-permute-start | bytes 1376264 | tf_op jit(solution)/shard_map/ppermute | solution.py:22
  23.1 19.6 %collective-permute-start.34 = (bf16[32,7168]{1,0:T(8,128)(2,1)}, bf16[32,7168]{1,0:T(8,128)(2,1)S(1)}, u32[]{:S(2)}, u32[]{:S(2)}) collective-permute-start(bf16[32,7168]{1,0:T(8,128)(2,1)} %collective-permute-done.33), channel_id=1, source_target_pairs={{4,2},{5,3},{2,0},{3,1},{12,10},{13,11},{10,8},{11,9},{20,18},{21,... | collective-permute-start | bytes 1376264 | tf_op jit(solution)/shard_map/ppermute | solution.py:22
  27.7 23.4 %collective-permute-start.2 = (bf16[32,7168]{1,0:T(8,128)(2,1)S(1)}, bf16[32,7168]{1,0:T(8,128)(2,1)S(1)}, u32[]{:S(2)}, u32[]{:S(2)}) collective-permute-start(bf16[32,7168]{1,0:T(8,128)(2,1)S(1)} %bitcast.78), channel_id=1, source_target_pairs={{2,0},{3,1},{4,2},{5,3},{6,4},{7,5},{10,8},{11,9},{12,10},{13,11},... | collective-permute-start | bytes 1376264 | tf_op jit(solution)/shard_map/ppermute | solution.py:22
  33.0 96.7 %collective-permute-start.50 = (bf16[32,7168]{1,0:T(8,128)(2,1)S(1)}, bf16[32,7168]{1,0:T(8,128)(2,1)}, u32[]{:S(2)}, u32[]{:S(2)}) collective-permute-start(bf16[32,7168]{1,0:T(8,128)(2,1)S(1)} %get-tuple-element.46), channel_id=1, source_target_pairs={{0,2},{1,3},{2,4},{3,5},{4,6},{5,7},{8,10},{9,11},{10,12},{11,13},... | collective-permute-start | bytes 1376264 | tf_op jit(solution)/shard_map/ppermute | solution.py:22
  42.7 24.2 %collective-permute-start.28 = (bf16[32,7168]{1,0:T(8,128)(2,1)}, bf16[32,7168]{1,0:T(8,128)(2,1)S(1)}, u32[]{:S(2)}, u32[]{:S(2)}) collective-permute-start(bf16[32,7168]{1,0:T(8,128)(2,1)} %collective-permute-done.27), channel_id=1, source_target_pairs={{4,2},{5,3},{2,0},{3,1},{12,10},{13,11},{10,8},{11,9},{20,18},{21,... | collective-permute-start | bytes 1376264 | tf_op jit(solution)/shard_map/ppermute | solution.py:22
  44.0 86.3 %collective-permute-start.52 = (bf16[32,7168]{1,0:T(8,128)(2,1)S(1)}, bf16[32,7168]{1,0:T(8,128)(2,1)}, u32[]{:S(2)}, u32[]{:S(2)}) collective-permute-start(bf16[32,7168]{1,0:T(8,128)(2,1)S(1)} %get-tuple-element.46), channel_id=1, source_target_pairs={{2,0},{3,1},{4,2},{5,3},{6,4},{7,5},{10,8},{11,9},{12,10},{13,11},... | collective-permute-start | bytes 1376264 | tf_op jit(solution)/shard_map/ppermute | solution.py:22
  51.7 34.8 %collective-permute-start.3 = (bf16[32,7168]{1,0:T(8,128)(2,1)S(1)}, bf16[32,7168]{1,0:T(8,128)(2,1)S(1)}, u32[]{:S(2)}, u32[]{:S(2)}) collective-permute-start(bf16[32,7168]{1,0:T(8,128)(2,1)S(1)} %collective-permute-done.2), channel_id=1, source_target_pairs={{4,2},{5,3},{2,0},{3,1},{12,10},{13,11},{10,8},{11,9},{20,18},{21,... | collective-permute-start | bytes 1376264 | tf_op jit(solution)/shard_map/ppermute | solution.py:22
  66.9 29.5 %collective-permute-start.35 = (bf16[32,7168]{1,0:T(8,128)(2,1)S(1)}, bf16[32,7168]{1,0:T(8,128)(2,1)S(1)}, u32[]{:S(2)}, u32[]{:S(2)}) collective-permute-start(bf16[32,7168]{1,0:T(8,128)(2,1)S(1)} %broadcast_select_fusion.12), channel_id=1, source_target_pairs={{4,6},{5,7},{2,0},{3,1},{12,14},{13,15},{10,8},{11,9},{20,22},{21,... | collective-permute-start | bytes 1376264 | tf_op jit(solution)/shard_map/ppermute | solution.py:22
  68.2 38.0 %collective-permute-start.29 = (bf16[32,7168]{1,0:T(8,128)(2,1)S(1)}, bf16[32,7168]{1,0:T(8,128)(2,1)S(1)}, u32[]{:S(2)}, u32[]{:S(2)}) collective-permute-start(bf16[32,7168]{1,0:T(8,128)(2,1)S(1)} %broadcast_select_fusion.13), channel_id=1, source_target_pairs={{4,6},{5,7},{2,0},{3,1},{12,14},{13,15},{10,8},{11,9},{20,22},{21,... | collective-permute-start | bytes 1376264 | tf_op jit(solution)/shard_map/ppermute | solution.py:22
  86.6 26.2 %collective-permute-start.4 = (bf16[32,7168]{1,0:T(8,128)(2,1)S(1)}, bf16[32,7168]{1,0:T(8,128)(2,1)S(1)}, u32[]{:S(2)}, u32[]{:S(2)}) collective-permute-start(bf16[32,7168]{1,0:T(8,128)(2,1)S(1)} %broadcast_select_fusion.15), channel_id=1, source_target_pairs={{4,6},{5,7},{2,0},{3,1},{12,14},{13,15},{10,8},{11,9},{20,22},{21,... | collective-permute-start | bytes 1376264 | tf_op jit(solution)/shard_map/ppermute | solution.py:22
  97.6 34.0 %collective-permute-start.36 = (bf16[128,7168]{1,0:T(8,128)(2,1)S(1)}, bf16[128,7168]{1,0:T(8,128)(2,1)}, u32[]{:S(2)}, u32[]{:S(2)}) collective-permute-start(bf16[128,7168]{1,0:T(8,128)(2,1)S(1)} %pad_maximum_fusion.3.refs_0_), channel_id=1, source_target_pairs={{0,1},{1,0},{2,3},{3,2},{4,5},{5,4},{6,7},{7,6},{8,9},{9,8},{10,11... | collective-permute-start | bytes 5505032 | tf_op jit(solution)/shard_map/ppermute | solution.py:26
  108.8 32.7 %collective-permute-start.30 = (bf16[128,7168]{1,0:T(8,128)(2,1)}, bf16[128,7168]{1,0:T(8,128)(2,1)}, u32[]{:S(2)}, u32[]{:S(2)}) collective-permute-start(bf16[128,7168]{1,0:T(8,128)(2,1)} %pad_maximum_fusion.2.refs_0_), channel_id=1, source_target_pairs={{0,1},{1,0},{2,3},{3,2},{4,5},{5,4},{6,7},{7,6},{8,9},{9,8},{10,11... | collective-permute-start | bytes 5505032 | tf_op jit(solution)/shard_map/ppermute | solution.py:26
  114.3 44.6 %collective-permute-start.5 = (bf16[128,7168]{1,0:T(8,128)(2,1)}, bf16[128,7168]{1,0:T(8,128)(2,1)}, u32[]{:S(2)}, u32[]{:S(2)}) collective-permute-start(bf16[128,7168]{1,0:T(8,128)(2,1)} %pad_maximum_fusion.refs_0_), channel_id=1, source_target_pairs={{0,1},{1,0},{2,3},{3,2},{4,5},{5,4},{6,7},{7,6},{8,9},{9,8},{10,11... | collective-permute-start | bytes 5505032 | tf_op jit(solution)/shard_map/ppermute | solution.py:26
  129.6 46.0 %collective-permute-start.51 = (bf16[32,7168]{1,0:T(8,128)(2,1)}, bf16[32,7168]{1,0:T(8,128)(2,1)S(1)}, u32[]{:S(2)}, u32[]{:S(2)}) collective-permute-start(bf16[32,7168]{1,0:T(8,128)(2,1)} %collective-permute-done.50), channel_id=1, source_target_pairs={{2,4},{3,5},{4,6},{5,7},{10,12},{11,13},{12,14},{13,15},{18,20},{1... | collective-permute-start | bytes 1376264 | tf_op jit(solution)/shard_map/ppermute | solution.py:22
  130.3 45.2 %collective-permute-start.53 = (bf16[32,7168]{1,0:T(8,128)(2,1)}, bf16[32,7168]{1,0:T(8,128)(2,1)S(1)}, u32[]{:S(2)}, u32[]{:S(2)}) collective-permute-start(bf16[32,7168]{1,0:T(8,128)(2,1)} %collective-permute-done.52), channel_id=1, source_target_pairs={{4,2},{5,3},{2,0},{3,1},{12,10},{13,11},{10,8},{11,9},{20,18},{21,... | collective-permute-start | bytes 1376264 | tf_op jit(solution)/shard_map/ppermute | solution.py:22
  175.6 76.0 %collective-permute-start.54 = (bf16[32,7168]{1,0:T(8,128)(2,1)S(1)}, bf16[32,7168]{1,0:T(8,128)(2,1)S(1)}, u32[]{:S(2)}, u32[]{:S(2)}) collective-permute-start(bf16[32,7168]{1,0:T(8,128)(2,1)S(1)} %broadcast_select_fusion.10), channel_id=1, source_target_pairs={{4,6},{5,7},{2,0},{3,1},{12,14},{13,15},{10,8},{11,9},{20,22},{21,... | collective-permute-start | bytes 1376264 | tf_op jit(solution)/shard_map/ppermute | solution.py:22
  182.9 20.2 %collective-permute-start.8 = (bf16[32,7168]{1,0:T(8,128)(2,1)S(1)}, bf16[32,7168]{1,0:T(8,128)(2,1)S(1)}, u32[]{:S(2)}, u32[]{:S(2)}) collective-permute-start(bf16[32,7168]{1,0:T(8,128)(2,1)S(1)} %broadcast_select_fusion.3), channel_id=1, source_target_pairs={{0,2},{1,3},{6,4},{7,5},{8,10},{9,11},{14,12},{15,13},{16,18},{17,... | collective-permute-start | bytes 1376264 | tf_op jit(solution)/shard_map/ppermute | solution.py:22
  193.3 19.6 %collective-permute-start.38 = (bf16[32,7168]{1,0:T(8,128)(2,1)S(1)}, bf16[32,7168]{1,0:T(8,128)(2,1)S(1)}, u32[]{:S(2)}, u32[]{:S(2)}) collective-permute-start(bf16[32,7168]{1,0:T(8,128)(2,1)S(1)} %get-tuple-element.41), channel_id=1, source_target_pairs={{0,2},{1,3},{6,4},{7,5},{8,10},{9,11},{14,12},{15,13},{16,18},{17,... | collective-permute-start | bytes 1376264 | tf_op jit(solution)/shard_map/ppermute | solution.py:22
  203.2 19.6 %collective-permute-start.7 = (bf16[32,7168]{1,0:T(8,128)(2,1)S(1)}, bf16[32,7168]{1,0:T(8,128)(2,1)S(1)}, u32[]{:S(2)}, u32[]{:S(2)}) collective-permute-start(bf16[32,7168]{1,0:T(8,128)(2,1)S(1)} %get-tuple-element.45), channel_id=1, source_target_pairs={{0,2},{1,3},{6,4},{7,5},{8,10},{9,11},{14,12},{15,13},{16,18},{17,... | collective-permute-start | bytes 1376264 | tf_op jit(solution)/shard_map/ppermute | solution.py:22
  213.1 19.5 %collective-permute-start.41 = (bf16[32,7168]{1,0:T(8,128)(2,1)S(1)}, bf16[32,7168]{1,0:T(8,128)(2,1)S(1)}, u32[]{:S(2)}, u32[]{:S(2)}) collective-permute-start(bf16[32,7168]{1,0:T(8,128)(2,1)S(1)} %get-tuple-element.32), channel_id=1, source_target_pairs={{0,2},{1,3},{2,4},{3,5},{4,6},{5,7},{8,10},{9,11},{10,12},{11,13},... | collective-permute-start | bytes 1376264 | tf_op jit(solution)/shard_map/ppermute | solution.py:22
  261.6 23.2 %collective-permute-start.47 = (bf16[32,7168]{1,0:T(8,128)(2,1)S(1)}, bf16[32,7168]{1,0:T(8,128)(2,1)S(1)}, u32[]{:S(2)}, u32[]{:S(2)}) collective-permute-start(bf16[32,7168]{1,0:T(8,128)(2,1)S(1)} %collective-permute-done.46), channel_id=1, source_target_pairs={{4,2},{5,3},{2,0},{3,1},{12,10},{13,11},{10,8},{11,9},{20,18},{21,... | collective-permute-start | bytes 1376264 | tf_op jit(solution)/shard_map/ppermute | solution.py:22
  263.0 49.5 %collective-permute-start.55 = (bf16[128,7168]{1,0:T(8,128)(2,1)S(1)}, bf16[128,7168]{1,0:T(8,128)(2,1)S(1)}, u32[]{:S(2)}, u32[]{:S(2)}) collective-permute-start(bf16[128,7168]{1,0:T(8,128)(2,1)S(1)} %pad_maximum_fusion.5.refs_0_), channel_id=1, source_target_pairs={{0,1},{1,0},{2,3},{3,2},{4,5},{5,4},{6,7},{7,6},{8,9},{9,8},{10,11... | collective-permute-start | bytes 5505032 | tf_op jit(solution)/shard_map/ppermute | solution.py:26
  274.9 19.7 %collective-permute-start.16 = (bf16[32,7168]{1,0:T(8,128)(2,1)S(1)}, bf16[32,7168]{1,0:T(8,128)(2,1)S(1)}, u32[]{:S(2)}, u32[]{:S(2)}) collective-permute-start(bf16[32,7168]{1,0:T(8,128)(2,1)S(1)} %collective-permute-done.15), channel_id=1, source_target_pairs={{4,2},{5,3},{2,0},{3,1},{12,10},{13,11},{10,8},{11,9},{20,18},{21,... | collective-permute-start | bytes 1376264 | tf_op jit(solution)/shard_map/ppermute | solution.py:22
  284.8 19.6 %collective-permute-start.48 = (bf16[32,7168]{1,0:T(8,128)(2,1)S(1)}, bf16[32,7168]{1,0:T(8,128)(2,1)S(1)}, u32[]{:S(2)}, u32[]{:S(2)}) collective-permute-start(bf16[32,7168]{1,0:T(8,128)(2,1)S(1)} %broadcast_select_fusion.11), channel_id=1, source_target_pairs={{4,6},{5,7},{2,0},{3,1},{12,14},{13,15},{10,8},{11,9},{20,22},{21,... | collective-permute-start | bytes 1376264 | tf_op jit(solution)/shard_map/ppermute | solution.py:22
  312.5 30.8 %collective-permute-start.18 = (bf16[128,7168]{1,0:T(8,128)(2,1)S(1)}, bf16[128,7168]{1,0:T(8,128)(2,1)}, u32[]{:S(2)}, u32[]{:S(2)}) collective-permute-start(bf16[128,7168]{1,0:T(8,128)(2,1)S(1)} %pad_maximum_fusion.1.refs_0_), channel_id=1, source_target_pairs={{0,1},{1,0},{2,3},{3,2},{4,5},{5,4},{6,7},{7,6},{8,9},{9,8},{10,11... | collective-permute-start | bytes 5505032 | tf_op jit(solution)/shard_map/ppermute | solution.py:26
  364.0 20.0 %collective-permute-start.21 = (bf16[32,7168]{1,0:T(8,128)(2,1)S(1)}, bf16[32,7168]{1,0:T(8,128)(2,1)S(1)}, u32[]{:S(2)}, u32[]{:S(2)}) collective-permute-start(bf16[32,7168]{1,0:T(8,128)(2,1)S(1)} %broadcast_select_fusion.2), channel_id=1, source_target_pairs={{0,2},{1,3},{6,4},{7,5},{8,10},{9,11},{14,12},{15,13},{16,18},{17,... | collective-permute-start | bytes 1376264 | tf_op jit(solution)/shard_map/ppermute | solution.py:22
  374.3 19.6 %collective-permute-start.57 = (bf16[32,7168]{1,0:T(8,128)(2,1)S(1)}, bf16[32,7168]{1,0:T(8,128)(2,1)S(1)}, u32[]{:S(2)}, u32[]{:S(2)}) collective-permute-start(bf16[32,7168]{1,0:T(8,128)(2,1)S(1)} %get-tuple-element.39), channel_id=1, source_target_pairs={{0,2},{1,3},{6,4},{7,5},{8,10},{9,11},{14,12},{15,13},{16,18},{17,... | collective-permute-start | bytes 1376264 | tf_op jit(solution)/shard_map/ppermute | solution.py:22
  384.1 19.6 %collective-permute-start.20 = (bf16[32,7168]{1,0:T(8,128)(2,1)S(1)}, bf16[32,7168]{1,0:T(8,128)(2,1)S(1)}, u32[]{:S(2)}, u32[]{:S(2)}) collective-permute-start(bf16[32,7168]{1,0:T(8,128)(2,1)S(1)} %get-tuple-element.43), channel_id=1, source_target_pairs={{0,2},{1,3},{6,4},{7,5},{8,10},{9,11},{14,12},{15,13},{16,18},{17,... | collective-permute-start | bytes 1376264 | tf_op jit(solution)/shard_map/ppermute | solution.py:22
  394.0 19.5 %collective-permute-start.60 = (bf16[32,7168]{1,0:T(8,128)(2,1)S(1)}, bf16[32,7168]{1,0:T(8,128)(2,1)S(1)}, u32[]{:S(2)}, u32[]{:S(2)}) collective-permute-start(bf16[32,7168]{1,0:T(8,128)(2,1)S(1)} %get-tuple-element.30), channel_id=1, source_target_pairs={{0,2},{1,3},{2,4},{3,5},{4,6},{5,7},{8,10},{9,11},{10,12},{11,13},... | collective-permute-start | bytes 1376264 | tf_op jit(solution)/shard_map/ppermute | solution.py:22
  403.9 19.2 %collective-permute-start.23 = (bf16[32,7168]{1,0:T(8,128)(2,1)S(1)}, bf16[32,7168]{1,0:T(8,128)(2,1)S(1)}, u32[]{:S(2)}, u32[]{:S(2)}) collective-permute-start(bf16[32,7168]{1,0:T(8,128)(2,1)S(1)} %get-tuple-element.34), channel_id=1, source_target_pairs={{0,2},{1,3},{2,4},{3,5},{4,6},{5,7},{8,10},{9,11},{10,12},{11,13},... | collective-permute-start | bytes 1376264 | tf_op jit(solution)/shard_map/ppermute | solution.py:22
  (50 other events, 779.5 us)

commit v2 on v0

v2 whole, which is shorter than its diff:
```python
import jax
import jax.numpy as jnp
from jax import lax
from jax.experimental import pallas as pl
from jax.experimental.pallas import tpu as pltpu
from jax.sharding import PartitionSpec as P

SLICES = 2
TICKS = 2
TOPK = 2
LINE = 4
LANES = 128
TILE = 1024
AHEAD = 6
VMEM_LIMIT = 48 * 1024 * 1024
F32 = jnp.float32
BF16 = jnp.bfloat16
NT = (((1,), (1,)), ((), ()))
TN = (((0,), (0,)), ((), ()))


def on_line():
    return lax.axis_size("expert") == LINE * SLICES


def hop(x, step):
    devices = lax.axis_size("expert")
    return lax.ppermute(x, "expert", [(i, i ^ (SLICES * step)) for i in range(devices)])


def swap(x):
    return lax.ppermute(x, "expert", [(i, i ^ 1) for i in range(lax.axis_size("expert"))])


def turned(x, turn):
    sections = lax.axis_size("section")
    return lax.ppermute(x, "section", [(i, (i + turn) % sections) for i in range(sections)])


def after(x, *others):
    return lax.optimization_barrier((x, *others))[0] if others else x


def beside(results, *others):
    return list(lax.optimization_barrier((*results, *others)))[: len(results)] if others else list(results)


def capacity_of(rows):
    experts = lax.axis_size("expert") // SLICES
    return min(rows, 3 * rows * TOPK // (2 * experts))


def slot_tables(table):
    mine = jnp.concatenate([table] + [hop(table, k) for k in range(1, LINE)], axis=0)
    both = jnp.concatenate([mine, swap(mine)], axis=0)
    return both.reshape(SLICES * LINE, *table.shape)


def picks_of(levels, capacity):
    named = levels > 0
    place = jnp.cumsum(named.astype(jnp.int32), axis=-1) - 1
    places = jnp.arange(capacity)[:, None]
    return (named[..., None, :] & (place[..., None, :] == places)).astype(F32)


def gates_of_slots(table, everyone_here):
    rows = table.shape[0]
    capacity = capacity_of(rows)
    chip = lax.axis_index("expert") // SLICES
    experts = lax.axis_size("expert") // SLICES
    ways = 2 * TICKS
    levels = everyone_here[:, :, : ways * experts].astype(F32)
    levels = levels.reshape(SLICES * LINE, rows, ways, experts).transpose(2, 3, 0, 1)
    sums = jnp.maximum(jnp.sum(levels, axis=1), 1.0)
    is_mine = (jnp.arange(experts) == chip)[None, :, None, None]
    here = jnp.sum(jnp.where(is_mine, levels, 0.0), axis=1)
    gates = here / sums
    packed = jnp.sum(picks_of(here, capacity) * gates[:, :, None, :], axis=-1)
    pad = jnp.zeros((ways, slot_rows(rows) - rows - (LINE - 1) * capacity), F32)
    column = []
    for core in range(SLICES):
        at = core * LINE
        column += [gates[:, at], *[packed[:, at + k] for k in range(1, LINE)], pad]
    column = jnp.concatenate(column, axis=1)[:, :, None]
    return [[column[d * TICKS + t] for t in range(TICKS)] for d in range(2)]


def picks_away(table):
    rows = table.shape[0]
    chip = lax.axis_index("expert") // SLICES
    experts = lax.axis_size("expert") // SLICES
    own = table[:, : 2 * TICKS * experts].astype(F32).reshape(rows, 2 * TICKS, experts)
    chosen = (jnp.arange(experts)[None, :] == (chip ^ jnp.arange(1, LINE))[:, None]).astype(F32)
    away = jnp.sum(own[:, :, None] * chosen, axis=3).transpose(1, 2, 0)
    picks = picks_of(away, capacity_of(rows)).astype(BF16)
    return [[picks[d * TICKS + t] for t in range(TICKS)] for d in range(2)]


def slot_rows(rows):
    return -(-(rows + (LINE - 1) * capacity_of(rows)) // 16) * 16


def in_kernel(body, args, shapes, name):
    vmem = pl.BlockSpec(memory_space=pltpu.VMEM)
    return pl.pallas_call(
        body,
        in_specs=[vmem] * len(args),
        out_specs=[vmem] * len(shapes),
        out_shape=[pltpu.VMEM(shape, BF16) for shape in shapes],
        compiler_params=pltpu.CompilerParams(vmem_limit_bytes=VMEM_LIMIT // 4),
        cost_estimate=pl.CostEstimate(flops=0, bytes_accessed=0, transcendentals=0),
        name=name,
    )(*args)


def pack_kernel(x, picks, *outs):
    for i, out in enumerate(outs):
        for span in tiles(x.shape[1]):
            value = jnp.dot(picks[i], x[:, span], preferred_element_type=F32)
            out[:, span] = value.astype(BF16)


def join_kernel(*refs):
    blocks, out = refs[:-1], refs[-1]
    rows = sum(b.shape[0] for b in blocks)
    for span in tiles(out.shape[1]):
        parts = [b[:, span].astype(F32) for b in blocks]
        parts.append(jnp.zeros((out.shape[0] - rows, parts[0].shape[1]), F32))
        out[:, span] = jnp.concatenate(parts, axis=0).astype(BF16)


class Gather:
    def __init__(self, x, picks, *ready):
        self.own = x
        shape = (picks.shape[1], x.shape[1])
        packed = in_kernel(pack_kernel, [x, picks], [shape] * (LINE - 1), "pack")
        self.arrived = [hop(p, k + 1) for k, p in enumerate(beside(packed, *ready))]

    def blocks(self, *ready):
        rows, width = self.own.shape
        arrived = beside(self.arrived, *ready)
        (mine,) = in_kernel(join_kernel, [self.own, *arrived], [(slot_rows(rows), width)], "join")
        return [mine, swap(mine)]


class Give:
    def __init__(self, parts, residual, picks):
        self.residual, self.picks = residual, picks
        rows, capacity = residual.shape[0], picks.shape[1]
        part = parts[0] + swap(parts[1])
        self.own = part[:rows]
        starts = [rows + k * capacity for k in range(LINE - 1)]
        self.arrived = [hop(part[at : at + capacity], k + 1) for k, at in enumerate(starts)]

    def total(self, *ready):
        total = self.residual.astype(F32) + self.own.astype(F32)
        for pick, part in zip(self.picks, beside(self.arrived, *ready)):
            total += lax.dot_general(pick, part, TN, preferred_element_type=F32)
        return total.astype(BF16)


def silu_parts(pre):
    sig = jax.nn.sigmoid(pre)
    return sig, pre * sig


def backward_factors(pre_gate, pre_up, d_hidden):
    sig, silu = silu_parts(pre_gate)
    d_up = (d_hidden * silu).astype(BF16)
    d_gate = (d_hidden * pre_up * sig * (1.0 + pre_gate * (1.0 - sig))).astype(BF16)
    return d_gate, d_up


def tiles(width):
    tile = TILE if width % TILE == 0 else width
    return [slice(i, i + tile) for i in range(0, width, tile)]


class Stream:
    def __init__(self, groups):
        self.groups = list(groups)
        self.queue = [copy for group in self.groups for copy in group]
        self.start(AHEAD)

    def start(self, count):
        for copy in self.queue[:count]:
            copy.start()
        self.queue = self.queue[count:]

    def take(self):
        group = self.groups.pop(0)
        for copy in group:
            copy.wait()
        self.start(len(group))


def copies(src, dst, sems, axis):
    spans = tiles(src.shape[axis])
    at = (lambda s: (s, slice(None))) if axis == 0 else (lambda s: (slice(None), s))
    return [pltpu.make_async_copy(src.at[at(s)], dst.at[at(s)], sems.at[i]) for i, s in enumerate(spans)]


def rows_in(blocks, x, sems):
    r = blocks[0].shape[0]
    done = [
        pltpu.make_async_copy(b.at[:, : x.shape[1]], x.at[i * r : (i + 1) * r], sems.at[i])
        for i, b in enumerate(blocks)
    ]
    for copy in done:
        copy.start()
    return done


def split_store(value, outs, span):
    r = outs[0].shape[0]
    for i, o in enumerate(outs):
        o[:, span] = value[i * r : (i + 1) * r].astype(BF16)


def forward_kernel(n, *refs):
    blocks, (gate, wg, wu, wd), outs = refs[:n], refs[n : n + 4], refs[n + 4 : 2 * n + 4]
    x, g, u, d, acc_gate, acc_up, s_in, s_g, s_u, s_d = refs[2 * n + 4 :]
    arriving = rows_in(blocks, x, s_in)
    pairs = [list(p) for p in zip(copies(wg, g, s_g, 0), copies(wu, u, s_u, 0))]
    stream = Stream(pairs + [[c] for c in copies(wd, d, s_d, 1)])
    for copy in arriving:
        copy.wait()
    for i, span in enumerate(tiles(g.shape[0])):
        stream.take()
        for w, acc in ((g, acc_gate), (u, acc_up)):
            value = jnp.dot(x[:, span], w[span, :], preferred_element_type=F32)
            acc[...] = value if i == 0 else acc[...] + value
    hidden = (silu_parts(acc_gate[...])[1] * gate[...] * acc_up[...]).astype(BF16)
    for span in tiles(d.shape[1]):
        stream.take()
        split_store(jnp.dot(hidden, d[:, span], preferred_element_type=F32), outs, span)


def pre_kernel(n, *refs):
    blocks, (wg, wu, pre_gate, pre_up) = refs[:n], refs[n : n + 4]
    x, g, u, s_in, s_g, s_u = refs[n + 4 :]
    arriving = rows_in(blocks, x, s_in)
    pairs = [list(p) for p in zip(copies(wg, g, s_g, 0), copies(wu, u, s_u, 0))]
    stream = Stream(pairs)
    for copy in arriving:
        copy.wait()
    for i, span in enumerate(tiles(g.shape[0])):
        stream.take()
        for w, acc in ((g, pre_gate), (u, pre_up)):
            value = jnp.dot(x[:, span], w[span, :], preferred_element_type=F32)
            acc[...] = value if i == 0 else acc[...] + value


def backward_kernel(n, *refs):
    blocks, (gate, pre_gate, pre_up, wg, wu, wd) = refs[:n], refs[n : n + 6]
    outs = refs[n + 6 : 2 * n + 6]
    x, g, u, d, acc, s_in, s_g, s_u, s_d = refs[2 * n + 6 :]
    arriving = rows_in(blocks, x, s_in)
    pairs = [list(p) for p in zip(copies(wg, g, s_g, 0), copies(wu, u, s_u, 0))]
    stream = Stream([[c] for c in copies(wd, d, s_d, 1)] + pairs)
    for copy in arriving:
        copy.wait()
    for i, span in enumerate(tiles(d.shape[1])):
        stream.take()
        value = lax.dot_general(x[:, span], d[:, span], NT, preferred_element_type=F32)
        acc[...] = value if i == 0 else acc[...] + value
    d_gate, d_up = backward_factors(pre_gate[...], pre_up[...], acc[...] * gate[...])
    for span in tiles(g.shape[0]):
        stream.take()
        value = lax.dot_general(d_gate, g[span, :], NT, preferred_element_type=F32)
        value += lax.dot_general(d_up, u[span, :], NT, preferred_element_type=F32)
        split_store(value, outs, span)


def call(kernel, n, args, in_vmem, out_shape, scratch, dots, name):
    anywhere, vmem = pl.BlockSpec(memory_space=pl.ANY), pl.BlockSpec(memory_space=pltpu.VMEM)
    weight = args[-1].size
    return pl.pallas_call(
        lambda *refs: kernel(n, *refs),
        in_specs=[vmem if i in in_vmem else anywhere for i in range(len(args))],
        out_specs=[pl.BlockSpec(memory_space=o.memory_space) for o in out_shape],
        out_shape=out_shape,
        scratch_shapes=scratch,
        compiler_params=pltpu.CompilerParams(vmem_limit_bytes=VMEM_LIMIT),
        cost_estimate=pl.CostEstimate(
            flops=0,
            bytes_accessed=0,
            transcendentals=0,
        ),
        name=name,
    )(*args)


def scratch_of(rows, weights, accs, n):
    width, hid = weights[0].shape
    dma = pltpu.SemaphoreType.DMA
    buffers = [pltpu.VMEM((rows, width), BF16)] + [pltpu.VMEM(w.shape, BF16) for w in weights]
    buffers += [pltpu.VMEM((rows, hid), F32)] * accs
    return buffers + [dma((n,))] + [dma((len(tiles(width)),)) for _ in weights]


def forward_piece(blocks, gate, wg, wu, wd):
    n, r, width = len(blocks), blocks[0].shape[0], wg.shape[0]
    return call(
        forward_kernel,
        n,
        [*blocks, gate, wg, wu, wd],
        (n,),
        [pltpu.VMEM((r, width), BF16)] * n,
        scratch_of(n * r, (wg, wu, wd), 2, n),
        3,
        "forward_piece",
    )


def pre_piece(blocks, wg, wu):
    n, r = len(blocks), blocks[0].shape[0]
    shape = pltpu.VMEM((n * r, wg.shape[1]), F32)
    scratch = scratch_of(n * r, (wg, wu), 0, n)
    return call(pre_kernel, n, [*blocks, wg, wu], (), [shape, shape], scratch, 2, "pre_piece")


def backward_piece(blocks, gate, pre, wg, wu, wd):
    n, r, width = len(blocks), blocks[0].shape[0], wg.shape[0]
    return call(
        backward_kernel,
        n,
        [*blocks, gate, *pre, wg, wu, wd],
        (n, n + 1, n + 2),
        [pltpu.VMEM((r, width), BF16)] * n,
        scratch_of(n * r, (wg, wu, wd), 1, n),
        3,
        "backward_piece",
    )


def level_table(route_ids, gate_levels, token_counts):
    section = lax.axis_index("section")
    sections = lax.axis_size("section")
    experts = lax.axis_size("expert") // SLICES
    routes, levels = route_ids[:, 0], gate_levels[:, 0]
    rows = routes.shape[2]
    first = lambda d, at: lax.dynamic_slice(token_counts[d, :, 0], (at,), (TICKS,))
    counts = jnp.stack([first(0, sections - 1 - section), first(1, section)])
    live = jnp.arange(rows)[None, None, :] < counts[:, :, None]
    named = (routes[..., None] == jnp.arange(experts)) & live[..., None, None]
    table = jnp.sum(jnp.where(named, levels[..., None], 0), axis=3)
    table = jnp.moveaxis(table, 2, 0).reshape(rows, -1).astype(BF16)
    return jnp.pad(table, ((0, 0), (0, -table.shape[1] % LANES)))


def gates_of(tables):
    devices = lax.axis_size("expert")
    experts = devices // SLICES
    mine = lax.axis_index("expert") // SLICES
    levels = tables[:, : 2 * TICKS * experts].astype(F32).reshape(-1, 2 * TICKS, experts)
    sums = jnp.maximum(jnp.sum(levels, axis=2), 1.0)
    own = jnp.sum(jnp.where(jnp.arange(experts) == mine, levels, 0.0), axis=2)
    gates = own / sums
    return [[gates[:, d * TICKS + t][:, None] for t in range(TICKS)] for d in range(2)]


def relay(x, entering, end, turn):
    return jnp.where(lax.axis_index("section") == end, entering, x), turn


def everyone(x):
    return lax.all_gather(x, "expert", axis=0, tiled=True)


def summed(parts, residual):
    parts = lax.psum_scatter(parts, "expert", scatter_dimension=0, tiled=True)
    return (residual.astype(F32) + parts.astype(F32)).astype(BF16)


def whole_line(fwd, bwd, saved, weights, tables, fwd_entering, bwd_entering):
    last = lax.axis_size("section") - 1
    (f_picks0, f_picks1), (b_picks0, b_picks1) = picks_away(tables)
    slots = slot_tables(tables)
    s0, g0 = Gather(saved[0], b_picks0, slots), Gather(bwd, b_picks0, slots)
    f_gates, b_gates = gates_of_slots(tables, slots)
    x0 = Gather(fwd, f_picks0, *s0.arrived)
    pre = pre_piece(s0.blocks(), *weights[:2])
    parts = backward_piece(g0.blocks(), b_gates[0], pre, *weights)
    parts = beside(parts, *x0.arrived)
    b0 = Give(parts, bwd, b_picks0)
    parts = forward_piece(x0.blocks(*parts), f_gates[0], *weights)
    f0 = Give(beside(parts, *b0.arrived), fwd, f_picks0)
    s1 = Gather(saved[1], b_picks1, *b0.arrived)
    b_out0 = b0.total()
    bwd1 = turned(*relay(b_out0, bwd_entering[0], 0, -1))
    g1 = Gather(bwd1, b_picks1, *f0.arrived)
    f_out0 = f0.total()
    fwd1 = turned(*relay(f_out0, fwd_entering[0], last, 1))
    pre = pre_piece(s1.blocks(fwd1), *weights[:2])
    x1 = Gather(fwd1, f_picks1, *s1.arrived)
    parts = backward_piece(g1.blocks(), b_gates[1], pre, *weights)
    parts = beside(parts, *x1.arrived)
    b1 = Give(parts, bwd1, b_picks1)
    parts = forward_piece(x1.blocks(*parts), f_gates[1], *weights)
    f1 = Give(beside(parts, *b1.arrived), fwd1, f_picks1)
    return [f_out0, f1.total()], [b_out0, b1.total()]


def plain(fwd, bwd, saved, weights, tables, fwd_entering, bwd_entering):
    wg, wu, wd = weights
    last = lax.axis_size("section") - 1

    def dot(a, b):
        return jnp.dot(a, b, preferred_element_type=F32)

    def dot_nt(a, b):
        return lax.dot_general(a, b, NT, preferred_element_type=F32)

    gates = gates_of(everyone(tables))
    fwd_list, bwd_list = [], []
    for tick in range(TICKS):
        x, s, g = everyone(fwd), everyone(saved[tick]), everyone(bwd)
        hidden = silu_parts(dot(x, wg))[1] * gates[0][tick] * dot(x, wu)
        fwd_list.append(summed(dot(hidden.astype(BF16), wd).astype(BF16), fwd))
        d_hidden = dot_nt(g, wd) * gates[1][tick]
        d_gate, d_up = backward_factors(dot(s, wg), dot(s, wu), d_hidden)
        back = dot_nt(d_gate, wg) + dot_nt(d_up, wu)
        bwd_list.append(summed(back.astype(BF16), bwd))
        if tick + 1 < TICKS:
            fwd = turned(*relay(fwd_list[-1], fwd_entering[tick], last, 1))
            bwd = turned(*relay(bwd_list[-1], bwd_entering[tick], 0, -1))
    return fwd_list, bwd_list


def local(
    fwd_arriving,
    fwd_entering,
    bwd_arriving,
    bwd_entering,
    saved_inputs,
    w_gate,
    w_up,
    w_down,
    route_ids,
    gate_levels,
    token_counts,
):
    run = whole_line if on_line() else plain
    fwd_list, bwd_list = run(
        fwd_arriving[0],
        bwd_arriving[0],
        saved_inputs[0],
        (w_gate[0, 0], w_up[0, 0], w_down[0, 0]),
        level_table(route_ids, gate_levels, token_counts),
        fwd_entering,
        bwd_entering,
    )
    return jnp.stack(fwd_list)[None], jnp.stack(bwd_list)[None]


def solution(mesh):
    return jax.shard_map(
        local,
        mesh=mesh,
        in_specs=(
            P("section", "expert", None),
            P(None, "expert", None),
            P("section", "expert", None),
            P(None, "expert", None),
            P("section", None, "expert", None),
            P("section", "expert", None, None),
            P("section", "expert", None, None),
            P("section", "expert", None, None),
            P(None, "section", None, "expert", None),
            P(None, "section", None, "expert", None),
            P(None, None, "expert"),
        ),
        out_specs=(P("section", None, "expert", None), P("section", None, "expert", None)),
        check_vma=False,
    )
```

time: 727 us -> 365 us (0.50)
  the two profiles are of different devices: /device:TPU:0 before, /device:TPU:8 now
where the time goes in v2:
time: 365 us; the launch traced here: 360 us
  waiting for transfers between devices  215 us (59%)
  Pallas kernels  67.3 us (18%)
  starting transfers between devices  47.2 us (13%)
  matrix products  11.6 us (3%)
  local copies, waits for them, and re-layouts  9.34 us (3%)
  other arithmetic  7.98 us (2%)
    ppermute x33, waiting for transfers between devices, hop(): lax.ppermute(x, 'expert', [(i, i ^ SLICES * step) for i in range(devices)])  211 us
    pallas_call x6, Pallas kernels, call(): pl.pallas_call(lambda *refs: kernel(n, *refs), in_specs=[vmem if i in in_...  60.5 us
    ppermute x33, starting transfers between devices, hop(): lax.ppermute(x, 'expert', [(i, i ^ SLICES * step) for i in range(devices)])  41.8 us
    dot_general x12, matrix products, total(): total += lax.dot_general(pick, part, TN, preferred_element_type=F32)  11.6 us
  transfers between devices with their start and end apart: 46, of which 26 were waited for; matrix products, arithmetic and copies ran while one was open for 6% of the time, Pallas kernels for 19%

profile of v2, /device:TPU:8, one launch (start us, length us, event | category | flops | bytes accessed | tf_op | source)
XLA Modules:
  0.0 360.1 jit_solution(6273958120866418414)
XLA Ops:
  2.3 3.0 collective-permute-start.1
  11.2 3.1 collective-permute-start.4
  16.4 2.9 collective-permute-start.10
  19.3 8.8 %collective-permute-done.4.refs_1_ = bf16[24,7168]{1,0:T(8,128)(2,1)S(1)} collective-permute-done((bf16[24,7168]{1,0:T(8,128)(2,1)S(1)}, bf16[24,7168]{1,0:T(8,128)(2,1)S(1)}, u32[]{:S(2)}, u32[]{:S(2)}) %collective-permute-start.4) | collective-permute-done | bytes 344096 | tf_op jit(solution)/shard_map/ppermute | solution.py:28
  29.6 8.6 %collective-permute-done.5.refs_2_ = bf16[24,7168]{1,0:T(8,128)(2,1)S(1)} collective-permute-done((bf16[24,7168]{1,0:T(8,128)(2,1)S(1)}, bf16[24,7168]{1,0:T(8,128)(2,1)S(1)}, u32[]{:S(2)}, u32[]{:S(2)}) %collective-permute-start.5) | collective-permute-done | bytes 344096 | tf_op jit(solution)/shard_map/ppermute | solution.py:28
  38.2 24.1 %collective-permute-done.6.refs_3_ = bf16[24,7168]{1,0:T(8,128)(2,1)S(1)} collective-permute-done((bf16[24,7168]{1,0:T(8,128)(2,1)S(1)}, bf16[24,7168]{1,0:T(8,128)(2,1)S(1)}, u32[]{:S(2)}, u32[]{:S(2)}) %collective-permute-start.6) | collective-permute-done | bytes 344096 | tf_op jit(solution)/shard_map/ppermute | solution.py:28
  62.4 5.2 %collective-permute-done.11.refs_2_ = bf16[24,7168]{1,0:T(8,128)(2,1)S(1)} collective-permute-done((bf16[24,7168]{1,0:T(8,128)(2,1)S(1)}, bf16[24,7168]{1,0:T(8,128)(2,1)S(1)}, u32[]{:S(2)}, u32[]{:S(2)}) %collective-permute-start.11) | collective-permute-done | bytes 344096 | tf_op jit(solution)/shard_map/ppermute | solution.py:28
  67.7 8.5 %collective-permute-done.12.refs_3_ = bf16[24,7168]{1,0:T(8,128)(2,1)S(1)} collective-permute-done((bf16[24,7168]{1,0:T(8,128)(2,1)S(1)}, bf16[24,7168]{1,0:T(8,128)(2,1)S(1)}, u32[]{:S(2)}, u32[]{:S(2)}) %collective-permute-start.12) | collective-permute-done | bytes 344096 | tf_op jit(solution)/shard_map/ppermute | solution.py:28
  84.2 7.2 %pre_piece.2 = (f32[224,512]{1,0:T(8,128)S(1)}, f32[224,512]{1,0:T(8,128)S(1)}) custom-call(bf16[112,7168]{1,0:T(8,128)(2,1)S(1)} %join.7.refs_0_, bf16[112,7168]{1,0:T(8,128)(2,1)} %collective-permute-done.14.refs_1_, bf16[7168,512]{1,0:T(8,128)(2,1)} %bitcast.136, bf16[7168,512]{1,0:T(8,128)(2,1)} %bitcast.142), custom_call_target="tpu_custom_call" | custom-call | tf_op jit(solution)/shard_map/pre_piece/pallas_call | solution.py:278
  91.4 12.2 %backward_piece.2 = (bf16[112,7168]{1,0:T(8,128)(2,1)S(1)}, bf16[112,7168]{1,0:T(8,128)(2,1)S(1)}) custom-call(bf16[112,7168]{1,0:T(8,128)(2,1)S(1)} %join.6.refs_0_, bf16[112,7168]{1,0:T(8,128)(2,1)} %collective-permute-done.13.refs_1_, f32[224,1]{1,0:T(8,128)S(1)} %copy.59.refs_2_, f32[224,512]{1,0:T(8,128)S(1)} %get-tuple-element.85.refs_3_, ...), custom_call_target="tpu_custom_call" | custom-call | tf_op jit(solution)/shard_map/backward_piece/pallas_call | solution.py:278
  105.9 8.6 %collective-permute-done.9.refs_3_ = bf16[24,7168]{1,0:T(8,128)(2,1)} collective-permute-done((bf16[24,7168]{1,0:T(8,128)(2,1)}, bf16[24,7168]{1,0:T(8,128)(2,1)}, u32[]{:S(2)}, u32[]{:S(2)}) %collective-permute-start.9) | collective-permute-done | bytes 344096 | tf_op jit(solution)/shard_map/ppermute | solution.py:28
  123.0 11.5 %forward_piece.2 = (bf16[112,7168]{1,0:T(8,128)(2,1)S(1)}, bf16[112,7168]{1,0:T(8,128)(2,1)}) custom-call(bf16[112,7168]{1,0:T(8,128)(2,1)S(1)} %join.8.refs_0_, bf16[112,7168]{1,0:T(8,128)(2,1)} %collective-permute-done.15.refs_1_, f32[224,1]{1,0:T(8,128)S(1)} %copy.60.refs_2_, bf16[7168,512]{1,0:T(8,128)(2,1)} %bitcast.138, bf16[7168,512]{1,0:T(8,128)(2,1)} %bitcast.144, ...), custom_call_target="tpu_custom_call" | custom-call | tf_op jit(solution)/shard_map/forward_piece/pallas_call | solution.py:278
  135.8 9.2 %collective-permute-done.18 = bf16[24,7168]{1,0:T(8,128)(2,1)} collective-permute-done((bf16[24,7168]{1,0:T(8,128)(2,1)}, bf16[24,7168]{1,0:T(8,128)(2,1)}, u32[]{:S(2)}, u32[]{:S(2)}) %collective-permute-start.18) | collective-permute-done | bytes 344096 | tf_op jit(solution)/shard_map/ppermute | solution.py:28
  144.9 8.2 %collective-permute-done.19 = bf16[24,7168]{1,0:T(8,128)(2,1)} collective-permute-done((bf16[24,7168]{1,0:T(8,128)(2,1)}, bf16[24,7168]{1,0:T(8,128)(2,1)}, u32[]{:S(2)}, u32[]{:S(2)}) %collective-permute-start.19) | collective-permute-done | bytes 344096 | tf_op jit(solution)/shard_map/ppermute | solution.py:28
  163.3 2.3 bitcast_select_fusion
  165.6 2.5 collective-permute-start.31
  168.1 17.5 %collective-permute-done.22 = bf16[24,7168]{1,0:T(8,128)(2,1)S(1)} collective-permute-done((bf16[24,7168]{1,0:T(8,128)(2,1)S(1)}, bf16[24,7168]{1,0:T(8,128)(2,1)S(1)}, u32[]{:S(2)}, u32[]{:S(2)}) %collective-permute-start.22) | collective-permute-done | bytes 344096 | tf_op jit(solution)/shard_map/ppermute | solution.py:28
  187.7 14.6 %collective-permute-done.23 = bf16[24,7168]{1,0:T(8,128)(2,1)S(1)} collective-permute-done((bf16[24,7168]{1,0:T(8,128)(2,1)S(1)}, bf16[24,7168]{1,0:T(8,128)(2,1)S(1)}, u32[]{:S(2)}, u32[]{:S(2)}) %collective-permute-start.23) | collective-permute-done | bytes 344096 | tf_op jit(solution)/shard_map/ppermute | solution.py:28
  210.7 21.4 %collective-permute-done.27.refs_3_ = bf16[24,7168]{1,0:T(8,128)(2,1)S(1)} collective-permute-done((bf16[24,7168]{1,0:T(8,128)(2,1)S(1)}, bf16[24,7168]{1,0:T(8,128)(2,1)S(1)}, u32[]{:S(2)}, u32[]{:S(2)}) %collective-permute-start.27) | collective-permute-done | bytes 344096 | tf_op jit(solution)/shard_map/ppermute | solution.py:28
  232.3 7.3 %collective-permute-done.33.refs_2_ = bf16[24,7168]{1,0:T(8,128)(2,1)S(1)} collective-permute-done((bf16[24,7168]{1,0:T(8,128)(2,1)S(1)}, bf16[24,7168]{1,0:T(8,128)(2,1)S(1)}, u32[]{:S(2)}, u32[]{:S(2)}) %collective-permute-start.33) | collective-permute-done | bytes 344096 | tf_op jit(solution)/shard_map/ppermute | solution.py:28
  239.6 8.8 %collective-permute-done.34.refs_3_ = bf16[24,7168]{1,0:T(8,128)(2,1)S(1)} collective-permute-done((bf16[24,7168]{1,0:T(8,128)(2,1)S(1)}, bf16[24,7168]{1,0:T(8,128)(2,1)S(1)}, u32[]{:S(2)}, u32[]{:S(2)}) %collective-permute-start.34) | collective-permute-done | bytes 344096 | tf_op jit(solution)/shard_map/ppermute | solution.py:28
  253.6 7.4 %pre_piece.3 = (f32[224,512]{1,0:T(8,128)S(1)}, f32[224,512]{1,0:T(8,128)S(1)}) custom-call(bf16[112,7168]{1,0:T(8,128)(2,1)S(1)} %join.10.refs_0_, bf16[112,7168]{1,0:T(8,128)(2,1)} %collective-permute-done.36.refs_1_, bf16[7168,512]{1,0:T(8,128)(2,1)} %bitcast.139, bf16[7168,512]{1,0:T(8,128)(2,1)} %bitcast.145), custom_call_target="tpu_custom_call" | custom-call | tf_op jit(solution)/shard_map/pre_piece/pallas_call | solution.py:278
  261.1 11.7 %backward_piece.3 = (bf16[112,7168]{1,0:T(8,128)(2,1)S(1)}, bf16[112,7168]{1,0:T(8,128)(2,1)S(1)}) custom-call(bf16[112,7168]{1,0:T(8,128)(2,1)S(1)} %join.9.refs_0_, bf16[112,7168]{1,0:T(8,128)(2,1)} %collective-permute-done.35.refs_1_, f32[224,1]{1,0:T(8,128)S(1)} %copy.61.refs_2_, f32[224,512]{1,0:T(8,128)S(1)} %get-tuple-element.119.refs_3_, ...), custom_call_target="tpu_custom_call" | custom-call | tf_op jit(solution)/shard_map/backward_piece/pallas_call | solution.py:278
  272.7 2.7 collective-permute-done.29.refs_2_
  275.4 8.6 %collective-permute-done.30.refs_3_ = bf16[24,7168]{1,0:T(8,128)(2,1)} collective-permute-done((bf16[24,7168]{1,0:T(8,128)(2,1)}, bf16[24,7168]{1,0:T(8,128)(2,1)}, u32[]{:S(2)}, u32[]{:S(2)}) %collective-permute-start.30) | collective-permute-done | bytes 344096 | tf_op jit(solution)/shard_map/ppermute | solution.py:28
  292.5 10.4 %forward_piece.3 = (bf16[112,7168]{1,0:T(8,128)(2,1)S(1)}, bf16[112,7168]{1,0:T(8,128)(2,1)S(1)}) custom-call(bf16[112,7168]{1,0:T(8,128)(2,1)S(1)} %join.11.refs_0_, bf16[112,7168]{1,0:T(8,128)(2,1)} %collective-permute-done.37.refs_1_, f32[224,1]{1,0:T(8,128)S(1)} %copy.62.refs_2_, bf16[7168,512]{1,0:T(8,128)(2,1)} %bitcast.141, ...), custom_call_target="tpu_custom_call" | custom-call | tf_op jit(solution)/shard_map/forward_piece/pallas_call | solution.py:278
  305.0 2.4 collective-permute-done.39
  307.5 12.7 %collective-permute-done.41 = bf16[24,7168]{1,0:T(8,128)(2,1)} collective-permute-done((bf16[24,7168]{1,0:T(8,128)(2,1)}, bf16[24,7168]{1,0:T(8,128)(2,1)}, u32[]{:S(2)}, u32[]{:S(2)}) %collective-permute-start.41) | collective-permute-done | bytes 344096 | tf_op jit(solution)/shard_map/ppermute | solution.py:28
  324.6 3.1 collective-permute-start.44
  329.1 10.8 %collective-permute-done.43 = bf16[24,7168]{1,0:T(8,128)(2,1)S(1)} collective-permute-done((bf16[24,7168]{1,0:T(8,128)(2,1)S(1)}, bf16[24,7168]{1,0:T(8,128)(2,1)S(1)}, u32[]{:S(2)}, u32[]{:S(2)}) %collective-permute-start.43) | collective-permute-done | bytes 344096 | tf_op jit(solution)/shard_map/ppermute | solution.py:28
  340.2 10.7 %collective-permute-done.44 = bf16[24,7168]{1,0:T(8,128)(2,1)S(1)} collective-permute-done((bf16[24,7168]{1,0:T(8,128)(2,1)S(1)}, bf16[24,7168]{1,0:T(8,128)(2,1)S(1)}, u32[]{:S(2)}, u32[]{:S(2)}) %collective-permute-start.44) | collective-permute-done | bytes 344096 | tf_op jit(solution)/shard_map/ppermute | solution.py:28
  351.2 7.2 %collective-permute-done.45 = bf16[24,7168]{1,0:T(8,128)(2,1)S(1)} collective-permute-done((bf16[24,7168]{1,0:T(8,128)(2,1)S(1)}, bf16[24,7168]{1,0:T(8,128)(2,1)S(1)}, u32[]{:S(2)}, u32[]{:S(2)}) %collective-permute-start.45) | collective-permute-done | bytes 344096 | tf_op jit(solution)/shard_map/ppermute | solution.py:28
  (181 shorter events, 75.1 us)
Async XLA Ops:
  11.2 16.9 %collective-permute-start.4 = (bf16[24,7168]{1,0:T(8,128)(2,1)S(1)}, bf16[24,7168]{1,0:T(8,128)(2,1)S(1)}, u32[]{:S(2)}, u32[]{:S(2)}) collective-permute-start(bf16[24,7168]{1,0:T(8,128)(2,1)S(1)} %get-tuple-element.73), channel_id=1, source_target_pairs={{0,2},{1,3},{2,0},{3,1},{4,6},{5,7},{6,4},{7,5},{8,10},{9,11},{10,... | collective-permute-start | bytes 1032200 | tf_op jit(solution)/shard_map/ppermute | solution.py:28
  14.8 23.3 %collective-permute-start.5 = (bf16[24,7168]{1,0:T(8,128)(2,1)S(1)}, bf16[24,7168]{1,0:T(8,128)(2,1)S(1)}, u32[]{:S(2)}, u32[]{:S(2)}) collective-permute-start(bf16[24,7168]{1,0:T(8,128)(2,1)S(1)} %get-tuple-element.74), channel_id=1, source_target_pairs={{0,4},{1,5},{2,6},{3,7},{4,0},{5,1},{6,2},{7,3},{8,12},{9,13},{10,... | collective-permute-start | bytes 1032200 | tf_op jit(solution)/shard_map/ppermute | solution.py:28
  14.9 47.3 %collective-permute-start.6 = (bf16[24,7168]{1,0:T(8,128)(2,1)S(1)}, bf16[24,7168]{1,0:T(8,128)(2,1)S(1)}, u32[]{:S(2)}, u32[]{:S(2)}) collective-permute-start(bf16[24,7168]{1,0:T(8,128)(2,1)S(1)} %get-tuple-element.75), channel_id=1, source_target_pairs={{0,6},{1,7},{2,4},{3,5},{4,2},{5,3},{6,0},{7,1},{8,14},{9,15},{10,... | collective-permute-start | bytes 1032200 | tf_op jit(solution)/shard_map/ppermute | solution.py:28
  16.4 46.0 %collective-permute-start.10 = (bf16[24,7168]{1,0:T(8,128)(2,1)S(1)}, bf16[24,7168]{1,0:T(8,128)(2,1)S(1)}, u32[]{:S(2)}, u32[]{:S(2)}) collective-permute-start(bf16[24,7168]{1,0:T(8,128)(2,1)S(1)} %get-tuple-element.82), channel_id=1, source_target_pairs={{0,2},{1,3},{2,0},{3,1},{4,6},{5,7},{6,4},{7,5},{8,10},{9,11},{10,... | collective-permute-start | bytes 1032200 | tf_op jit(solution)/shard_map/ppermute | solution.py:28
  19.3 48.4 %collective-permute-start.11 = (bf16[24,7168]{1,0:T(8,128)(2,1)S(1)}, bf16[24,7168]{1,0:T(8,128)(2,1)S(1)}, u32[]{:S(2)}, u32[]{:S(2)}) collective-permute-start(bf16[24,7168]{1,0:T(8,128)(2,1)S(1)} %get-tuple-element.83), channel_id=1, source_target_pairs={{0,4},{1,5},{2,6},{3,7},{4,0},{5,1},{6,2},{7,3},{8,12},{9,13},{10,... | collective-permute-start | bytes 1032200 | tf_op jit(solution)/shard_map/ppermute | solution.py:28
  28.1 48.1 %collective-permute-start.12 = (bf16[24,7168]{1,0:T(8,128)(2,1)S(1)}, bf16[24,7168]{1,0:T(8,128)(2,1)S(1)}, u32[]{:S(2)}, u32[]{:S(2)}) collective-permute-start(bf16[24,7168]{1,0:T(8,128)(2,1)S(1)} %get-tuple-element.84), channel_id=1, source_target_pairs={{0,6},{1,7},{2,4},{3,5},{4,2},{5,3},{6,0},{7,1},{8,14},{9,15},{10,... | collective-permute-start | bytes 1032200 | tf_op jit(solution)/shard_map/ppermute | solution.py:28
  62.4 21.8 %collective-permute-start.14 = (bf16[112,7168]{1,0:T(8,128)(2,1)S(1)}, bf16[112,7168]{1,0:T(8,128)(2,1)}, u32[]{:S(2)}, u32[]{:S(2)}) collective-permute-start(bf16[112,7168]{1,0:T(8,128)(2,1)S(1)} %join.7.refs_0_), channel_id=1, source_target_pairs={{0,1},{1,0},{2,3},{3,2},{4,5},{5,4},{6,7},{7,6},{8,9},{9,8},{10,11... | collective-permute-start | bytes 4816904 | tf_op jit(solution)/shard_map/ppermute | solution.py:32
  80.3 23.3 %collective-permute-start.7 = (bf16[24,7168]{1,0:T(8,128)(2,1)}, bf16[24,7168]{1,0:T(8,128)(2,1)}, u32[]{:S(2)}, u32[]{:S(2)}) collective-permute-start(bf16[24,7168]{1,0:T(8,128)(2,1)} %copy-done.16), channel_id=1, source_target_pairs={{0,2},{1,3},{2,0},{3,1},{4,6},{5,7},{6,4},{7,5},{8,10},{9,11},{10,... | collective-permute-start | bytes 1032200 | tf_op jit(solution)/shard_map/ppermute | solution.py:28
  80.4 25.5 %collective-permute-start.8 = (bf16[24,7168]{1,0:T(8,128)(2,1)}, bf16[24,7168]{1,0:T(8,128)(2,1)}, u32[]{:S(2)}, u32[]{:S(2)}) collective-permute-start(bf16[24,7168]{1,0:T(8,128)(2,1)} %copy-done.15), channel_id=1, source_target_pairs={{0,4},{1,5},{2,6},{3,7},{4,0},{5,1},{6,2},{7,3},{8,12},{9,13},{10,... | collective-permute-start | bytes 1032200 | tf_op jit(solution)/shard_map/ppermute | solution.py:28
  82.4 32.1 %collective-permute-start.9 = (bf16[24,7168]{1,0:T(8,128)(2,1)}, bf16[24,7168]{1,0:T(8,128)(2,1)}, u32[]{:S(2)}, u32[]{:S(2)}) collective-permute-start(bf16[24,7168]{1,0:T(8,128)(2,1)} %copy-done.14), channel_id=1, source_target_pairs={{0,6},{1,7},{2,4},{3,5},{4,2},{5,3},{6,0},{7,1},{8,14},{9,15},{10,... | collective-permute-start | bytes 1032200 | tf_op jit(solution)/shard_map/ppermute | solution.py:28
  119.4 16.4 %collective-permute-start.17 = (bf16[24,7168]{1,0:T(8,128)(2,1)}, bf16[24,7168]{1,0:T(8,128)(2,1)}, u32[]{:S(2)}, u32[]{:S(2)}) collective-permute-start(bf16[24,7168]{1,0:T(8,128)(2,1)} %get-tuple-element.149), channel_id=1, source_target_pairs={{0,2},{1,3},{2,0},{3,1},{4,6},{5,7},{6,4},{7,5},{8,10},{9,11},{10,... | collective-permute-start | bytes 1032200 | tf_op jit(solution)/shard_map/ppermute | solution.py:28
  119.4 25.5 %collective-permute-start.18 = (bf16[24,7168]{1,0:T(8,128)(2,1)}, bf16[24,7168]{1,0:T(8,128)(2,1)}, u32[]{:S(2)}, u32[]{:S(2)}) collective-permute-start(bf16[24,7168]{1,0:T(8,128)(2,1)} %get-tuple-element.148), channel_id=1, source_target_pairs={{0,4},{1,5},{2,6},{3,7},{4,0},{5,1},{6,2},{7,3},{8,12},{9,13},{10,... | collective-permute-start | bytes 1032200 | tf_op jit(solution)/shard_map/ppermute | solution.py:28
  121.4 31.7 %collective-permute-start.19 = (bf16[24,7168]{1,0:T(8,128)(2,1)}, bf16[24,7168]{1,0:T(8,128)(2,1)}, u32[]{:S(2)}, u32[]{:S(2)}) collective-permute-start(bf16[24,7168]{1,0:T(8,128)(2,1)} %get-tuple-element.147), channel_id=1, source_target_pairs={{0,6},{1,7},{2,4},{3,5},{4,2},{5,3},{6,0},{7,1},{8,14},{9,15},{10,... | collective-permute-start | bytes 1032200 | tf_op jit(solution)/shard_map/ppermute | solution.py:28
  153.6 53.5 %collective-permute-start.25 = (bf16[24,7168]{1,0:T(8,128)(2,1)S(1)}, bf16[24,7168]{1,0:T(8,128)(2,1)S(1)}, u32[]{:S(2)}, u32[]{:S(2)}) collective-permute-start(bf16[24,7168]{1,0:T(8,128)(2,1)S(1)} %get-tuple-element.104), channel_id=1, source_target_pairs={{0,2},{1,3},{2,0},{3,1},{4,6},{5,7},{6,4},{7,5},{8,10},{9,11},{10,... | collective-permute-start | bytes 1032200 | tf_op jit(solution)/shard_map/ppermute | solution.py:28
  153.7 55.4 %collective-permute-start.26 = (bf16[24,7168]{1,0:T(8,128)(2,1)S(1)}, bf16[24,7168]{1,0:T(8,128)(2,1)S(1)}, u32[]{:S(2)}, u32[]{:S(2)}) collective-permute-start(bf16[24,7168]{1,0:T(8,128)(2,1)S(1)} %get-tuple-element.105), channel_id=1, source_target_pairs={{0,4},{1,5},{2,6},{3,7},{4,0},{5,1},{6,2},{7,3},{8,12},{9,13},{10,... | collective-permute-start | bytes 1032200 | tf_op jit(solution)/shard_map/ppermute | solution.py:28
  158.9 26.7 %collective-permute-start.22 = (bf16[24,7168]{1,0:T(8,128)(2,1)S(1)}, bf16[24,7168]{1,0:T(8,128)(2,1)S(1)}, u32[]{:S(2)}, u32[]{:S(2)}) collective-permute-start(bf16[24,7168]{1,0:T(8,128)(2,1)S(1)} %get-tuple-element.145), channel_id=1, source_target_pairs={{0,4},{1,5},{2,6},{3,7},{4,0},{5,1},{6,2},{7,3},{8,12},{9,13},{10,... | collective-permute-start | bytes 1032200 | tf_op jit(solution)/shard_map/ppermute | solution.py:28
  161.3 26.1 %collective-permute-start.21 = (bf16[24,7168]{1,0:T(8,128)(2,1)S(1)}, bf16[24,7168]{1,0:T(8,128)(2,1)S(1)}, u32[]{:S(2)}, u32[]{:S(2)}) collective-permute-start(bf16[24,7168]{1,0:T(8,128)(2,1)S(1)} %get-tuple-element.146), channel_id=1, source_target_pairs={{0,2},{1,3},{2,0},{3,1},{4,6},{5,7},{6,4},{7,5},{8,10},{9,11},{10,... | collective-permute-start | bytes 1032200 | tf_op jit(solution)/shard_map/ppermute | solution.py:28
  165.6 40.9 %collective-permute-start.31 = (bf16[32,7168]{1,0:T(8,128)(2,1)S(1)}, bf16[32,7168]{1,0:T(8,128)(2,1)S(1)}, u32[]{:S(2)}, u32[]{:S(2)}) collective-permute-start(bf16[32,7168]{1,0:T(8,128)(2,1)S(1)} %get-tuple-element.174), channel_id=1, source_target_pairs={{0,24},{8,0},{16,8},{24,16},{1,25},{9,1},{17,9},{25,17},{2,26},{10... | collective-permute-start | bytes 1376264 | tf_op jit(solution)/shard_map/ppermute | solution.py:37
  185.6 16.8 %collective-permute-start.23 = (bf16[24,7168]{1,0:T(8,128)(2,1)S(1)}, bf16[24,7168]{1,0:T(8,128)(2,1)S(1)}, u32[]{:S(2)}, u32[]{:S(2)}) collective-permute-start(bf16[24,7168]{1,0:T(8,128)(2,1)S(1)} %get-tuple-element.144), channel_id=1, source_target_pairs={{0,6},{1,7},{2,4},{3,5},{4,2},{5,3},{6,0},{7,1},{8,14},{9,15},{10,... | collective-permute-start | bytes 1032200 | tf_op jit(solution)/shard_map/ppermute | solution.py:28
  203.6 28.5 %collective-permute-start.24 = (bf16[32,7168]{1,0:T(8,128)(2,1)S(1)}, bf16[32,7168]{1,0:T(8,128)(2,1)S(1)}, u32[]{:S(2)}, u32[]{:S(2)}) collective-permute-start(bf16[32,7168]{1,0:T(8,128)(2,1)S(1)} %get-tuple-element.172), channel_id=1, source_target_pairs={{0,8},{8,16},{16,24},{24,0},{1,9},{9,17},{17,25},{25,1},{2,10},{10... | collective-permute-start | bytes 1376264 | tf_op jit(solution)/shard_map/ppermute | solution.py:37
  205.1 27.0 %collective-permute-start.27 = (bf16[24,7168]{1,0:T(8,128)(2,1)S(1)}, bf16[24,7168]{1,0:T(8,128)(2,1)S(1)}, u32[]{:S(2)}, u32[]{:S(2)}) collective-permute-start(bf16[24,7168]{1,0:T(8,128)(2,1)S(1)} %get-tuple-element.106), channel_id=1, source_target_pairs={{0,6},{1,7},{2,4},{3,5},{4,2},{5,3},{6,0},{7,1},{8,14},{9,15},{10,... | collective-permute-start | bytes 1032200 | tf_op jit(solution)/shard_map/ppermute | solution.py:28
  207.1 25.2 %collective-permute-start.32 = (bf16[24,7168]{1,0:T(8,128)(2,1)S(1)}, bf16[24,7168]{1,0:T(8,128)(2,1)S(1)}, u32[]{:S(2)}, u32[]{:S(2)}) collective-permute-start(bf16[24,7168]{1,0:T(8,128)(2,1)S(1)} %get-tuple-element.113), channel_id=1, source_target_pairs={{0,2},{1,3},{2,0},{3,1},{4,6},{5,7},{6,4},{7,5},{8,10},{9,11},{10,... | collective-permute-start | bytes 1032200 | tf_op jit(solution)/shard_map/ppermute | solution.py:28
  207.2 32.4 %collective-permute-start.33 = (bf16[24,7168]{1,0:T(8,128)(2,1)S(1)}, bf16[24,7168]{1,0:T(8,128)(2,1)S(1)}, u32[]{:S(2)}, u32[]{:S(2)}) collective-permute-start(bf16[24,7168]{1,0:T(8,128)(2,1)S(1)} %get-tuple-element.114), channel_id=1, source_target_pairs={{0,4},{1,5},{2,6},{3,7},{4,0},{5,1},{6,2},{7,3},{8,12},{9,13},{10,... | collective-permute-start | bytes 1032200 | tf_op jit(solution)/shard_map/ppermute | solution.py:28
  209.1 39.3 %collective-permute-start.34 = (bf16[24,7168]{1,0:T(8,128)(2,1)S(1)}, bf16[24,7168]{1,0:T(8,128)(2,1)S(1)}, u32[]{:S(2)}, u32[]{:S(2)}) collective-permute-start(bf16[24,7168]{1,0:T(8,128)(2,1)S(1)} %get-tuple-element.115), channel_id=1, source_target_pairs={{0,6},{1,7},{2,4},{3,5},{4,2},{5,3},{6,0},{7,1},{8,14},{9,15},{10,... | collective-permute-start | bytes 1032200 | tf_op jit(solution)/shard_map/ppermute | solution.py:28
  232.2 21.4 %collective-permute-start.36 = (bf16[112,7168]{1,0:T(8,128)(2,1)S(1)}, bf16[112,7168]{1,0:T(8,128)(2,1)}, u32[]{:S(2)}, u32[]{:S(2)}) collective-permute-start(bf16[112,7168]{1,0:T(8,128)(2,1)S(1)} %join.10.refs_0_), channel_id=1, source_target_pairs={{0,1},{1,0},{2,3},{3,2},{4,5},{5,4},{6,7},{7,6},{8,9},{9,8},{10,11... | collective-permute-start | bytes 4816904 | tf_op jit(solution)/shard_map/ppermute | solution.py:32
  250.0 22.8 %collective-permute-start.28 = (bf16[24,7168]{1,0:T(8,128)(2,1)}, bf16[24,7168]{1,0:T(8,128)(2,1)}, u32[]{:S(2)}, u32[]{:S(2)}) collective-permute-start(bf16[24,7168]{1,0:T(8,128)(2,1)} %get-tuple-element.107), channel_id=1, source_target_pairs={{0,2},{1,3},{2,0},{3,1},{4,6},{5,7},{6,4},{7,5},{8,10},{9,11},{10,... | collective-permute-start | bytes 1032200 | tf_op jit(solution)/shard_map/ppermute | solution.py:28
  250.0 25.5 %collective-permute-start.29 = (bf16[24,7168]{1,0:T(8,128)(2,1)}, bf16[24,7168]{1,0:T(8,128)(2,1)}, u32[]{:S(2)}, u32[]{:S(2)}) collective-permute-start(bf16[24,7168]{1,0:T(8,128)(2,1)} %get-tuple-element.108), channel_id=1, source_target_pairs={{0,4},{1,5},{2,6},{3,7},{4,0},{5,1},{6,2},{7,3},{8,12},{9,13},{10,... | collective-permute-start | bytes 1032200 | tf_op jit(solution)/shard_map/ppermute | solution.py:28
  251.9 32.2 %collective-permute-start.30 = (bf16[24,7168]{1,0:T(8,128)(2,1)}, bf16[24,7168]{1,0:T(8,128)(2,1)}, u32[]{:S(2)}, u32[]{:S(2)}) collective-permute-start(bf16[24,7168]{1,0:T(8,128)(2,1)} %get-tuple-element.109), channel_id=1, source_target_pairs={{0,6},{1,7},{2,4},{3,5},{4,2},{5,3},{6,0},{7,1},{8,14},{9,15},{10,... | collective-permute-start | bytes 1032200 | tf_op jit(solution)/shard_map/ppermute | solution.py:28
  288.9 18.5 %collective-permute-start.39 = (bf16[24,7168]{1,0:T(8,128)(2,1)}, bf16[24,7168]{1,0:T(8,128)(2,1)}, u32[]{:S(2)}, u32[]{:S(2)}) collective-permute-start(bf16[24,7168]{1,0:T(8,128)(2,1)} %get-tuple-element.143), channel_id=1, source_target_pairs={{0,2},{1,3},{2,0},{3,1},{4,6},{5,7},{6,4},{7,5},{8,10},{9,11},{10,... | collective-permute-start | bytes 1032200 | tf_op jit(solution)/shard_map/ppermute | solution.py:28
  290.8 29.3 %collective-permute-start.41 = (bf16[24,7168]{1,0:T(8,128)(2,1)}, bf16[24,7168]{1,0:T(8,128)(2,1)}, u32[]{:S(2)}, u32[]{:S(2)}) collective-permute-start(bf16[24,7168]{1,0:T(8,128)(2,1)} %get-tuple-element.141), channel_id=1, source_target_pairs={{0,6},{1,7},{2,4},{3,5},{4,2},{5,3},{6,0},{7,1},{8,14},{9,15},{10,... | collective-permute-start | bytes 1032200 | tf_op jit(solution)/shard_map/ppermute | solution.py:28
  324.6 26.3 %collective-permute-start.44 = (bf16[24,7168]{1,0:T(8,128)(2,1)S(1)}, bf16[24,7168]{1,0:T(8,128)(2,1)S(1)}, u32[]{:S(2)}, u32[]{:S(2)}) collective-permute-start(bf16[24,7168]{1,0:T(8,128)(2,1)S(1)} %get-tuple-element.139), channel_id=1, source_target_pairs={{0,4},{1,5},{2,6},{3,7},{4,0},{5,1},{6,2},{7,3},{8,12},{9,13},{10,... | collective-permute-start | bytes 1032200 | tf_op jit(solution)/shard_map/ppermute | solution.py:28
  328.7 29.7 %collective-permute-start.45 = (bf16[24,7168]{1,0:T(8,128)(2,1)S(1)}, bf16[24,7168]{1,0:T(8,128)(2,1)S(1)}, u32[]{:S(2)}, u32[]{:S(2)}) collective-permute-start(bf16[24,7168]{1,0:T(8,128)(2,1)S(1)} %get-tuple-element.138), channel_id=1, source_target_pairs={{0,6},{1,7},{2,4},{3,5},{4,2},{5,3},{6,0},{7,1},{8,14},{9,15},{10,... | collective-permute-start | bytes 1032200 | tf_op jit(solution)/shard_map/ppermute | solution.py:28
  (36 other events, 500.9 us)
